TPU v7x, 512 devices: a whole 4x4x16 slice. The times are simulated.
512 devices in a mesh: gx: 16 (over x_lo, y, core), gy: 16 (over z), gz: 2 (over x_hi).
Axes of the slice: x: 4 (x_hi: 2, x_lo: 2; x = x_hi * 2 + x_lo), y: 4, z: 16, core: 2. Of those that a mesh axis runs over, the one named last changes fastest.
Arguments:
- thermal_anomaly: float32 [256, 256, 256], P('gx', 'gy', 'gz'), may hold values from -6 to 6
- specific_vapour: float32 [256, 256, 256], P('gx', 'gy', 'gz'), may hold values from -6 to 6
- server_thermal_load: float32 [256, 256, 256], P('gx', 'gy', 'gz'), may hold values from -5 to 5
- lateral_mixing_coefficient: float32 [256, 256, 256], P('gx', 'gy', 'gz'), may hold values from 40 to 800
- upward_mixing_coefficient: float32 [256, 256, 256], P('gx', 'gy', 'gz'), may hold values from 0.1 to 0.25
- cfl_along_lateral_axis: float32 [256, 256, 256], P('gx', 'gy', 'gz'), may hold values from -30 to 30
- cfl_across_lateral_axis: float32 [256, 256, 256], P('gx', 'gy', 'gz'), may hold values from -30 to 30
- cfl_upward_axis: float32 [256, 256, 256], P('gx', 'gy', 'gz'), may hold values from -0.15 to 0.15
Outputs:
- temperature_new: float32 [256, 256, 256], P('gx', 'gy', 'gz')
- humidity_new: float32 [256, 256, 256], P('gx', 'gy', 'gz')
All inputs are finite; a program needn't handle non-finite values.
Results may differ from a plain program's by a relative error of at most 0.0003.
Values sent between devices are 32-bit elements; how exact they have to be, the bound alone decides.
A program may use at most 64 MiB of HBM per device.

v0:
```python
import jax
import jax.numpy as jnp
from jax import lax
from jax.sharding import PartitionSpec as P

vapour_scaling = 0.8


def extended(x, sides, width):
    edges = {}
    for axis, dim in sides:
        peers, length = (lax.axis_size(axis), x.shape[dim])
        up = [(i, (i + 1) % peers) for i in range(peers - 1)]
        last = lax.slice_in_dim(x, length - width, length, axis=dim)
        leading = lax.slice_in_dim(x, 0, width, axis=dim)
        edges[dim] = (
            lax.ppermute(last, axis, up),
            lax.ppermute(leading, axis, [(b, a) for a, b in up]),
        )
    done = []
    for _, dim in sides:
        low, high = edges[dim]
        around = [(width, width) if d in done else (0, 0) for d in range(x.ndim)]
        x = jnp.concatenate([jnp.pad(low, around), x, jnp.pad(high, around)], axis=dim)
        done.append(dim)
    return x


def bands(east_coef, west_coef):
    return (-west_coef, 1.0 + east_coef + west_coef, -east_coef)


def eliminate(lower_band, diagonal_band, upper_band, right_side, upper_in, right_in):

    def forward(carried, cell_data):
        upper_before, right_before = carried
        lower_cell, diagonal_cell, upper_cell, right_cell = cell_data
        pivots = diagonal_cell - lower_cell * upper_before
        upper_now = upper_cell / pivots
        right_now = (right_cell - lower_cell * right_before) / pivots
        return ((upper_now, right_now), (upper_now, right_now))

    unused, ratios = lax.scan(
        forward, (upper_in, right_in), (lower_band, diagonal_band, upper_band, right_side)
    )
    return ratios


def substitute(upper_ratios, right_ratios, value_in):

    def backward(value_after, cell_data):
        upper_ratio, right_ratio = cell_data
        value = right_ratio - upper_ratio * value_after
        return (value, value)

    unused, values = lax.scan(backward, value_in, (upper_ratios, right_ratios), reverse=True)
    return values


def whole_solve(east_coef, west_coef, right_side):
    lower_band, diagonal_band, upper_band = bands(east_coef, west_coef)
    zeros = jnp.zeros_like(right_side[0])
    upper_ratios, right_ratios = eliminate(
        lower_band, diagonal_band, upper_band, right_side, zeros, zeros
    )
    return substitute(upper_ratios, right_ratios, zeros)


def body(
    thermal_anomaly,
    specific_vapour,
    server_thermal_load,
    lateral_mixing_coefficient,
    upward_mixing_coefficient,
    cfl_along_lateral_axis,
    cfl_across_lateral_axis,
    cfl_upward_axis,
):
    tracer_bundle = jnp.stack([thermal_anomaly, specific_vapour])
    factors = jnp.array([1.0, vapour_scaling], jnp.float32).reshape(2, 1, 1, 1)
    weights = jnp.array([1.0, 0.0], jnp.float32).reshape(2, 1, 1, 1)
    source = weights * server_thermal_load[None]
    east_x = factors * lateral_mixing_coefficient[None] - 0.5 * cfl_along_lateral_axis[None]
    west_x = factors * lateral_mixing_coefficient[None] + 0.5 * cfl_along_lateral_axis[None]
    east_y = factors * lateral_mixing_coefficient[None] - 0.5 * cfl_across_lateral_axis[None]
    west_y = factors * lateral_mixing_coefficient[None] + 0.5 * cfl_across_lateral_axis[None]
    east_z = factors * upward_mixing_coefficient[None] - 0.5 * cfl_upward_axis[None]
    west_z = factors * upward_mixing_coefficient[None] + 0.5 * cfl_upward_axis[None]
    padded = extended(tracer_bundle, (("gy", 2), ("gz", 3)), 1)
    first_side = (
        tracer_bundle
        + (
            east_y * (padded[:, :, 2:, 1:-1] - tracer_bundle)
            + west_y * (padded[:, :, :-2, 1:-1] - tracer_bundle)
        )
        + (
            east_z * (padded[:, :, 1:-1, 2:] - tracer_bundle)
            + west_z * (padded[:, :, 1:-1, :-2] - tracer_bundle)
        )
        + source
    )
    packed = jnp.stack(
        [lateral_mixing_coefficient, cfl_along_lateral_axis, first_side[0], first_side[1]]
    )
    lines = lax.all_to_all(packed, "gx", split_axis=2, concat_axis=1, tiled=True)
    line_east = factors * lines[0][None] - 0.5 * lines[1][None]
    line_west = factors * lines[0][None] + 0.5 * lines[1][None]
    solved = whole_solve(
        jnp.moveaxis(line_east, 1, 0), jnp.moveaxis(line_west, 1, 0), jnp.moveaxis(lines[2:4], 1, 0)
    )
    half_field = lax.all_to_all(
        jnp.moveaxis(solved, 0, 1), "gx", split_axis=1, concat_axis=2, tiled=True
    )
    padded_half = extended(half_field, (("gx", 1), ("gz", 3)), 1)
    second_side = (
        half_field
        + (
            east_x * (padded_half[:, 2:, :, 1:-1] - half_field)
            + west_x * (padded_half[:, :-2, :, 1:-1] - half_field)
        )
        + (
            east_z * (padded_half[:, 1:-1, :, 2:] - half_field)
            + west_z * (padded_half[:, 1:-1, :, :-2] - half_field)
        )
        + source
    )
    packed_y = jnp.stack(
        [lateral_mixing_coefficient, cfl_across_lateral_axis, second_side[0], second_side[1]]
    )
    lines_y = lax.all_to_all(packed_y, "gy", split_axis=1, concat_axis=2, tiled=True)
    line_east_y = factors * lines_y[0][None] - 0.5 * lines_y[1][None]
    line_west_y = factors * lines_y[0][None] + 0.5 * lines_y[1][None]
    solved_y = whole_solve(
        jnp.moveaxis(line_east_y, 2, 0),
        jnp.moveaxis(line_west_y, 2, 0),
        jnp.moveaxis(lines_y[2:4], 2, 0),
    )
    new_fields = lax.all_to_all(
        jnp.moveaxis(solved_y, 0, 2), "gy", split_axis=2, concat_axis=1, tiled=True
    )
    return (new_fields[0], new_fields[1])


def solution(mesh):
    in_specs = (
        P("gx", "gy", "gz"),
        P("gx", "gy", "gz"),
        P("gx", "gy", "gz"),
        P("gx", "gy", "gz"),
        P("gx", "gy", "gz"),
        P("gx", "gy", "gz"),
        P("gx", "gy", "gz"),
        P("gx", "gy", "gz"),
    )
    out_specs = (P("gx", "gy", "gz"), P("gx", "gy", "gz"))
    return jax.shard_map(body, mesh=mesh, in_specs=in_specs, out_specs=out_specs, check_vma=False)
```

profile of v0, /device:TPU:24, one launch (start us, length us, event | category | flops | bytes accessed | tf_op | source)
XLA Modules:
  0.0 232.0 jit_solution(4281317001275695284)
XLA Ops:
  0.6 1.1 copy_bitcast_fusion.2
  1.7 0.1 fusion.41
  1.8 1.3 collective-permute-start.2
  3.1 0.0 copy-start.2
  3.1 6.2 %collective-permute-start.3 = (f32[2,16,16,1]{3,1,2,0:T(8,128)S(1)}, f32[2,16,16,1]{3,1,2,0:T(8,128)S(1)}, u32[]{:S(2)}, u32[]{:S(2)}) collective-permute-start(f32[2,16,16,1]{3,1,2,0:T(8,128)S(1)} %get-tuple-element.525), channel_id=1, source_target_pairs={{0,1},{2,3},{4,5},{6,7},{8,9},{10,11},{12,13},{14,15},{16,17},{18,... | collective-permute-start | bytes 6152 | tf_op jit(solution)/shard_map/ppermute | solution.py:17
  9.4 1.3 collective-permute-start
  10.7 0.0 copy-start.1
  10.7 4.7 %collective-permute-start.1 = (f32[2,16,1,128]{3,1,2,0:T(8,128)S(1)}, f32[2,16,1,128]{3,1,2,0:T(8,128)S(1)}, u32[]{:S(2)}, u32[]{:S(2)}) collective-permute-start(f32[2,16,1,128]{3,1,2,0:T(8,128)S(1)} %get-tuple-element.526), channel_id=1, source_target_pairs={{0,2},{2,4},{4,6},{6,8},{8,10},{10,12},{12,14},{14,16},{16,18},{18... | collective-permute-start | bytes 49160 | tf_op jit(solution)/shard_map/ppermute | solution.py:17
  15.4 0.0 copy-start.3
  15.4 0.9 copy-done.3
  16.4 0.0 copy-start.4
  16.4 0.8 copy-done.4
  17.3 0.9 copy-done.5
  18.3 0.8 copy-done
  19.2 0.6 copy-done.6
  19.8 0.0 copy-done.7
  19.8 0.3 multiply_add_fusion.3
  20.1 0.8 copy.93
  21.0 9.0 %all-to-all-start = ((f32[4,16,16,128]{3,1,0,2:T(8,128)}), f32[4,16,16,128]{3,1,0,2:T(8,128)S(1)}, u32[]{:S(2)}, u32[]{:S(2)}) async-start(f32[4,16,16,128]{3,1,0,2:T(8,128)} %copy.93), calls=%async_computation | async-start | bytes 1048576 | tf_op jit(solution)/shard_map/all_to_all | solution.py:105
  30.0 8.7 %all-to-all-done = f32[4,16,16,128]{3,1,0,2:T(8,128)S(1)} async-done(((f32[4,16,16,128]{3,1,0,2:T(8,128)}), f32[4,16,16,128]{3,1,0,2:T(8,128)S(1)}, u32[]{:S(2)}, u32[]{:S(2)}) %all-to-all-start) | async-done | bytes 524320 | tf_op jit(solution)/shard_map/all_to_all | solution.py:105
  38.8 0.2 copy.116
  39.0 0.4 fusion.34
  39.4 0.1 broadcast.144.clone.3
  39.5 0.1 broadcast.144.clone.4
  39.5 32.3 %while.68 = (s32[]{:T(128)}, f32[2,1,128]{2,1,0:T(1,128)S(1)}, f32[2,1,128]{2,1,0:T(1,128)S(1)}, f32[256,2,1,128]{3,1,2,0:T(2,128)S(1)}, f32[256,2,1,128]{3,1,2,...) while((s32[]{:T(128)}, f32[2,1,128]{2,1,0:T(1,128)S(1)}, ...), condition=%wide.region_1.2_spmd.clone, body=%wide.region_0.1_spmd.clone.sunk | while | flops 2051 | bytes 20619 | solution.py:43
  71.9 0.1 broadcast.144.clone.2
  72.0 17.8 %while.69 = (s32[]{:T(128)}, f32[2,1,128]{2,1,0:T(1,128)S(1)}, f32[256,2,1,128]{3,1,2,0:T(2,128)S(1)}, f32[256,2,1,128]{3,1,2,0:T(2,128)S(1)}, f32[256,2,1,128]{...) while((s32[]{:T(128)}, f32[2,1,128]{2,1,0:T(1,128)S(1)}, ...), condition=%wide.region_3.4_spmd.clone, body=%wide.region_2.3_spmd.clone.sunk | while | flops 772 | bytes 10355 | solution.py:56
  89.8 10.7 %all_to_all.51 = f32[2,256,1,128]{3,0,2,1:T(2,128)S(1)} all-to-all(f32[2,256,1,128]{3,0,2,1:T(2,128)S(1)} %bitcast.124), channel_id=1, replica_groups=mesh['gx'=16,'gy'=16,'gz'=2] {'gx'}, dimensions={1} | all-to-all | bytes 524288 | tf_op jit(solution)/shard_map/all_to_all | solution.py:111
  100.4 0.1 fusion.68
  100.6 1.3 collective-permute-start.6
  101.9 6.1 %collective-permute-start.7 = (f32[2,16,16,1]{3,1,2,0:T(8,128)S(1)}, f32[2,16,16,1]{3,1,2,0:T(8,128)S(1)}, u32[]{:S(2)}, u32[]{:S(2)}) collective-permute-start(f32[2,16,16,1]{3,1,2,0:T(8,128)S(1)} %get-tuple-element.521), channel_id=1, source_target_pairs={{0,1},{2,3},{4,5},{6,7},{8,9},{10,11},{12,13},{14,15},{16,17},{18,... | collective-permute-start | bytes 6152 | tf_op jit(solution)/shard_map/ppermute | solution.py:17
  108.0 1.9 collective-permute-start.4
  109.9 2.4 %collective-permute-start.5 = (f32[2,1,16,128]{3,1,2,0:T(1,128)S(1)}, f32[2,1,16,128]{3,1,2,0:T(1,128)S(1)}, u32[]{:S(2)}, u32[]{:S(2)}) collective-permute-start(f32[2,1,16,128]{3,1,2,0:T(1,128)S(1)} %get-tuple-element.522), channel_id=1, source_target_pairs={{0,32},{32,64},{64,96},{96,128},{128,160},{160,192},{192,224},{224... | collective-permute-start | bytes 49160 | tf_op jit(solution)/shard_map/ppermute | solution.py:17
  112.5 0.1 collective-permute-done.6
  112.5 1.2 collective-permute-done.7
  113.7 1.3 collective-permute-done.5
  115.0 0.4 multiply_add_fusion.2
  115.5 1.0 copy.98
  116.4 11.8 %all-to-all-start.2 = ((f32[4,16,16,128]{3,2,0,1:T(8,128)}), f32[4,16,16,128]{3,2,0,1:T(8,128)S(1)}, u32[]{:S(2)}, u32[]{:S(2)}) async-start(f32[4,16,16,128]{3,2,0,1:T(8,128)} %copy.98), calls=%async_computation.2 | async-start | bytes 1048576 | tf_op jit(solution)/shard_map/all_to_all | solution.py:130
  128.3 29.6 %all-to-all-done.2 = f32[4,16,16,128]{3,2,0,1:T(8,128)S(1)} async-done(((f32[4,16,16,128]{3,2,0,1:T(8,128)}), f32[4,16,16,128]{3,2,0,1:T(8,128)S(1)}, u32[]{:S(2)}, u32[]{:S(2)}) %all-to-all-start.2) | async-done | bytes 524320 | tf_op jit(solution)/shard_map/all_to_all | solution.py:130
  158.0 0.4 fusion.31
  158.3 0.1 broadcast.144.clone
  158.4 0.1 broadcast.144.clone.1
  158.5 29.2 %while.70 = (s32[]{:T(128)}, f32[2,1,128]{2,1,0:T(1,128)S(1)}, f32[2,1,128]{2,1,0:T(1,128)S(1)}, f32[256,2,1,128]{3,1,2,0:T(2,128)S(1)}, f32[256,2,1,128]{3,1,2,...) while((s32[]{:T(128)}, f32[2,1,128]{2,1,0:T(1,128)S(1)}, ...), condition=%wide.region_5.6_spmd.clone, body=%wide.region_4.5_spmd.clone.sunk | while | flops 2051 | bytes 18571 | solution.py:43
  187.7 0.1 broadcast.144
  187.8 17.8 %while.71 = (s32[]{:T(128)}, f32[2,1,128]{2,1,0:T(1,128)S(1)}, f32[256,2,1,128]{3,1,2,0:T(2,128)S(1)}, f32[256,2,1,128]{3,1,2,0:T(2,128)S(1)}, f32[256,2,1,128]{...) while((s32[]{:T(128)}, f32[2,1,128]{2,1,0:T(1,128)S(1)}, ...), condition=%wide.region_7.8_spmd.clone, body=%wide.region_6.7_spmd.clone.sunk | while | flops 772 | bytes 10355 | solution.py:56
  205.6 25.5 %all_to_all.52 = f32[2,1,256,128]{3,0,1,2:T(2,128)S(1)} all-to-all(f32[2,1,256,128]{3,0,1,2:T(2,128)S(1)} %bitcast.123), channel_id=1, replica_groups=mesh['gx'=16,'gy'=16,'gz'=2] {'gy'}, dimensions={2} | all-to-all | bytes 524288 | tf_op jit(solution)/shard_map/all_to_all | solution.py:138
  231.1 0.9 fusion.67
  (4392 shorter events, 53.6 us)
Async XLA Ops:
  1.8 17.4 %collective-permute-start.2 = (f32[2,16,16,1]{3,1,2,0:T(8,128)S(1)}, f32[2,16,16,1]{3,1,2,0:T(8,128)S(1)}, u32[]{:S(2)}, u32[]{:S(2)}) collective-permute-start(f32[2,16,16,1]{3,1,2,0:T(8,128)S(1)} %get-tuple-element.524), channel_id=1, source_target_pairs={{1,0},{3,2},{5,4},{7,6},{9,8},{11,10},{13,12},{15,14},{17,16},{19,... | collective-permute-start | bytes 6152 | tf_op jit(solution)/shard_map/ppermute | solution.py:18
  3.1 12.2 %copy-start.2 = (f32[16,16,128]{2,1,0:T(8,128)S(1)}, f32[16,16,128]{2,1,0:T(8,128)}, u32[]{:S(2)}) copy-start(f32[16,16,128]{2,1,0:T(8,128)} %param.25) | copy-start | bytes 393220
  3.1 16.1 %collective-permute-start.3 = (f32[2,16,16,1]{3,1,2,0:T(8,128)S(1)}, f32[2,16,16,1]{3,1,2,0:T(8,128)S(1)}, u32[]{:S(2)}, u32[]{:S(2)}) collective-permute-start(f32[2,16,16,1]{3,1,2,0:T(8,128)S(1)} %get-tuple-element.525), channel_id=1, source_target_pairs={{0,1},{2,3},{4,5},{6,7},{8,9},{10,11},{12,13},{14,15},{16,17},{18,... | collective-permute-start | bytes 6152 | tf_op jit(solution)/shard_map/ppermute | solution.py:17
  9.4 9.8 %collective-permute-start = (f32[2,16,1,128]{3,1,2,0:T(8,128)S(1)}, f32[2,16,1,128]{3,1,2,0:T(8,128)S(1)}, u32[]{:S(2)}, u32[]{:S(2)}) collective-permute-start(f32[2,16,1,128]{3,1,2,0:T(8,128)S(1)} %get-tuple-element.527), channel_id=1, source_target_pairs={{2,0},{4,2},{6,4},{8,6},{10,8},{12,10},{14,12},{16,14},{18,16},{20... | collective-permute-start | bytes 49160 | tf_op jit(solution)/shard_map/ppermute | solution.py:18
  10.7 4.7 %copy-start.1 = (f32[16,16,128]{2,1,0:T(8,128)S(1)}, f32[16,16,128]{2,1,0:T(8,128)}, u32[]{:S(2)}) copy-start(f32[16,16,128]{2,1,0:T(8,128)} %param.24) | copy-start | bytes 393220
  10.7 8.5 %collective-permute-start.1 = (f32[2,16,1,128]{3,1,2,0:T(8,128)S(1)}, f32[2,16,1,128]{3,1,2,0:T(8,128)S(1)}, u32[]{:S(2)}, u32[]{:S(2)}) collective-permute-start(f32[2,16,1,128]{3,1,2,0:T(8,128)S(1)} %get-tuple-element.526), channel_id=1, source_target_pairs={{0,2},{2,4},{4,6},{6,8},{8,10},{10,12},{12,14},{14,16},{16,18},{18... | collective-permute-start | bytes 49160 | tf_op jit(solution)/shard_map/ppermute | solution.py:17
  15.4 0.9 copy-start.3
  16.4 0.9 copy-start.4
  17.3 0.9 copy-start.5
  18.2 0.9 copy-start
  19.1 0.7 copy-start.6
  19.1 0.7 copy-start.7
  21.0 17.7 %all-to-all-start = ((f32[4,16,16,128]{3,1,0,2:T(8,128)}), f32[4,16,16,128]{3,1,0,2:T(8,128)S(1)}, u32[]{:S(2)}, u32[]{:S(2)}) async-start(f32[4,16,16,128]{3,1,0,2:T(8,128)} %copy.93), calls=%async_computation | async-start | bytes 1048576 | tf_op jit(solution)/shard_map/all_to_all | solution.py:105
  100.6 11.9 %collective-permute-start.6 = (f32[2,16,16,1]{3,1,2,0:T(8,128)S(1)}, f32[2,16,16,1]{3,1,2,0:T(8,128)S(1)}, u32[]{:S(2)}, u32[]{:S(2)}) collective-permute-start(f32[2,16,16,1]{3,1,2,0:T(8,128)S(1)} %get-tuple-element.520), channel_id=1, source_target_pairs={{1,0},{3,2},{5,4},{7,6},{9,8},{11,10},{13,12},{15,14},{17,16},{19,... | collective-permute-start | bytes 6152 | tf_op jit(solution)/shard_map/ppermute | solution.py:18
  101.9 11.8 %collective-permute-start.7 = (f32[2,16,16,1]{3,1,2,0:T(8,128)S(1)}, f32[2,16,16,1]{3,1,2,0:T(8,128)S(1)}, u32[]{:S(2)}, u32[]{:S(2)}) collective-permute-start(f32[2,16,16,1]{3,1,2,0:T(8,128)S(1)} %get-tuple-element.521), channel_id=1, source_target_pairs={{0,1},{2,3},{4,5},{6,7},{8,9},{10,11},{12,13},{14,15},{16,17},{18,... | collective-permute-start | bytes 6152 | tf_op jit(solution)/shard_map/ppermute | solution.py:17
  108.0 5.7 %collective-permute-start.4 = (f32[2,1,16,128]{3,1,2,0:T(1,128)S(1)}, f32[2,1,16,128]{3,1,2,0:T(1,128)S(1)}, u32[]{:S(2)}, u32[]{:S(2)}) collective-permute-start(f32[2,1,16,128]{3,1,2,0:T(1,128)S(1)} %get-tuple-element.523), channel_id=1, source_target_pairs={{32,0},{64,32},{96,64},{128,96},{160,128},{192,160},{224,192},{256... | collective-permute-start | bytes 49160 | tf_op jit(solution)/shard_map/ppermute | solution.py:18
  109.9 5.1 %collective-permute-start.5 = (f32[2,1,16,128]{3,1,2,0:T(1,128)S(1)}, f32[2,1,16,128]{3,1,2,0:T(1,128)S(1)}, u32[]{:S(2)}, u32[]{:S(2)}) collective-permute-start(f32[2,1,16,128]{3,1,2,0:T(1,128)S(1)} %get-tuple-element.522), channel_id=1, source_target_pairs={{0,32},{32,64},{64,96},{96,128},{128,160},{160,192},{192,224},{224... | collective-permute-start | bytes 49160 | tf_op jit(solution)/shard_map/ppermute | solution.py:17
  116.4 41.4 %all-to-all-start.2 = ((f32[4,16,16,128]{3,2,0,1:T(8,128)}), f32[4,16,16,128]{3,2,0,1:T(8,128)S(1)}, u32[]{:S(2)}, u32[]{:S(2)}) async-start(f32[4,16,16,128]{3,2,0,1:T(8,128)} %copy.98), calls=%async_computation.2 | async-start | bytes 1048576 | tf_op jit(solution)/shard_map/all_to_all | solution.py:130
where the time goes:
time: 233 us; the launch traced here: 232 us
  starting transfers between devices  46 us (20%)
  local copies, waits for them, and re-layouts  44.7 us (19%)
  loops' own time  44.2 us (19%)
  waiting for transfers between devices  40.8 us (18%)
  blocking collectives  36.1 us (15%)
  other arithmetic  19 us (8%)
    all_to_all x1, waiting for transfers between devices, body(): lax.all_to_all(packed_y, 'gy', split_axis=1, concat_axis=2, tiled=True)  29.6 us
    another operation x2, loops' own time, eliminate(): lax.scan(forward, (upper_in, right_in), (lower_band, diagonal_band, upper...  27.5 us
    all_to_all x1, blocking collectives, body(): lax.all_to_all(jnp.moveaxis(solved_y, 0, 2), 'gy', split_axis=2, concat_a...  25.5 us
    dynamic_slice x2304, local copies, waits for them, and re-layouts, eliminate(): lax.scan(forward, (upper_in, right_in), (lower_band, diagonal_band, upper...  21.2 us
    ppermute x4, starting transfers between devices, extended(): lax.ppermute(last, axis, up)  19.4 us
    another operation x2, loops' own time, substitute(): lax.scan(backward, value_in, (upper_ratios, right_ratios), reverse=True)  16.7 us
    dynamic_update_slice x1024, local copies, waits for them, and re-layouts, eliminate(): lax.scan(forward, (upper_in, right_in), (lower_band, diagonal_band, upper...  14.6 us
    all_to_all x1, starting transfers between devices, body(): lax.all_to_all(packed_y, 'gy', split_axis=1, concat_axis=2, tiled=True)  11.8 us

commit v1 on v0

v1 whole, which is shorter than its diff:
```python
import functools

import jax
import jax.numpy as jnp
from jax import lax
from jax.experimental import pallas as pl
from jax.experimental.pallas import tpu as pltpu
from jax.sharding import PartitionSpec as P

vapour_scaling = 0.8
N = 16
LANES = 128
SOLVERS = 4
MESH = pl.DeviceIdType.MESH
F32 = jnp.float32


def kernel(
    t_in, h_in, load_in, k_in, kz_in, cx_in, cy_in, cz_in,
    t_out, h_out,
    fields, load, mix, mix_z, cfl_x, cfl_y, cfl_z, result,
    side, mask_z, half,
    first_w, last_w, inv, wi, ratio_c, from_left, from_right, part,
    tmp_a, tmp_b,
    y_send, y_face, z_send, z_face,
    coef_send, coef_recv, side_send, side_recv, back_send, back_recv, lu,
    in_sem, out_sem, y_sem, z_sem, net_sem,
):
    gx, gy, gz = lax.axis_index("gx"), lax.axis_index("gy"), lax.axis_index("gz")
    core = lax.rem(gx, 2)

    tile_x = lax.rem(lax.div(gx, 2), 4)
    tile_y = lax.div(gy, 4)
    axes = (
        dict(
            me=gx, tile=tile_x, solves=gx == 8 * lax.rem(tile_x, 2) + 2 * tile_x,
            solver=lambda s: 8 * (s % 2) + 2 * s, device=lambda i: (i, gy, gz),
        ),
        dict(
            me=gy, tile=tile_y, solves=gy == 4 * tile_y + 2 * core,
            solver=lambda s: 4 * s + 2 * core, device=lambda i: (gx, i, gz),
        ),
    )

    barrier = pltpu.get_barrier_semaphore()

    def greet(device):
        pl.semaphore_signal(barrier, inc=1, device_id=device, device_id_type=MESH)

    greet((gx, gy, 1 - gz))
    expected = 1
    pl.when(gy > 0)(lambda: greet((gx, gy - 1, gz)))
    pl.when(gy < N - 1)(lambda: greet((gx, gy + 1, gz)))
    expected += jnp.where(gy > 0, 1, 0) + jnp.where(gy < N - 1, 1, 0)
    for ax in axes:
        for s in range(SOLVERS):
            pl.when(ax["me"] != ax["solver"](s))(
                functools.partial(greet, ax["device"](ax["solver"](s)))
            )

        @pl.when(ax["solves"])
        def _(ax=ax):
            @pl.loop(0, N)
            def _(i):
                pl.when(i != ax["me"])(lambda: greet(ax["device"](i)))

        expected += jnp.where(ax["solves"], N - 1 + SOLVERS - 1, SOLVERS)

    loads = [
        pltpu.make_async_copy(src, dst, in_sem.at[n])
        for n, (src, dst) in enumerate((
            (t_in, fields.at[0]), (h_in, fields.at[1]), (k_in, mix), (cx_in, cfl_x),
            (cy_in, cfl_y), (kz_in, mix_z), (cz_in, cfl_z), (load_in, load),
        ))
    ]
    for copy in loads:
        copy.start()

    lane = lax.broadcasted_iota(jnp.int32, (2, N, LANES), 2)
    field = lax.broadcasted_iota(jnp.int32, (2, N, LANES), 0)
    ratio = jnp.where(field == 0, 1.0, vapour_scaling).astype(F32)
    weight = jnp.where(field == 0, 1.0, 0.0).astype(F32)
    lane2 = lax.broadcasted_iota(jnp.int32, (N, LANES), 1)
    face = jnp.where(gz == 0, LANES - 1, 0)

    def along(n):
        return pl.ds(N * n, N)

    def across(n):
        return pl.ds(n, N, stride=N)

    def pair(ref, rows):
        return jnp.broadcast_to(ref[rows, :][None], (2, N, LANES))

    def pack_column(rows, y, packed):
        for f in range(2):
            n = 1 + N * f + y
            moved = pltpu.roll(rows[f], n + 1 - gz, 1)
            packed = jnp.where(lane2 == n, moved, packed)
        return packed

    def unpack_column(packed, y):
        return jnp.stack(
            [pltpu.roll(packed, LANES - 1 - (1 + N * f + y) + gz, 1) for f in range(2)]
        )

    loads[0].wait()
    loads[1].wait()
    y_send[0] = fields[:, across(0), :]
    y_send[1] = fields[:, across(N - 1), :]
    packed = jnp.zeros((N, LANES), F32)
    for y in range(N):
        packed = pack_column(fields[:, across(y), :], y, packed)
    z_send[0] = packed
    pl.when(gy == 0)(lambda: y_face.__setitem__(0, jnp.zeros((2, N, LANES), F32)))
    pl.when(gy == N - 1)(lambda: y_face.__setitem__(1, jnp.zeros((2, N, LANES), F32)))

    def factor(d, rows, cfl):
        def bands(k):
            mixed = ratio * pair(mix, rows(k))
            speed = 0.5 * pair(cfl, rows(k))
            return mixed - speed, mixed + speed

        rest, chain = None, None
        for k in range(N):
            east, west = bands(k)
            v = 1.0 + (west if rest is None else west * rest)
            i = 1.0 / (v + east)
            c = east * i
            rest = v * i
            w = west * i
            chain = w if chain is None else w * chain
            inv[d, k] = i
            wi[d, k] = w
            ratio_c[d, k] = c
            tmp_a[k] = chain
        q, t, prod = chain, c, None
        from_left[d, N - 1] = q
        from_right[d, N - 1] = t
        ends = [None, None, q, t]
        for k in range(N - 1, -1, -1):
            if k < N - 1:
                c = ratio_c[d, k]
                q = tmp_a[k] + c * q
                t = c * t
                from_left[d, k] = q
                from_right[d, k] = t
        ends[0], ends[1] = q, t
        for v, value in enumerate(ends):
            for s in range(SOLVERS):
                coef_send[d, s, v] = value[s // 2, 8 * (s % 2) : 8 * (s % 2) + 8]

    def weights(d, rows, cfl):
        def bands(k):
            mixed = ratio * pair(mix, rows(k))
            speed = 0.5 * pair(cfl, rows(k))
            return mixed - speed, mixed + speed

        rest, prod = None, None
        for k in range(N - 1, -1, -1):
            east, west = bands(k)
            v = 1.0 + (east if rest is None else east * rest)
            i = 1.0 / (v + west)
            rest = v * i
            tmp_a[k] = i
            tmp_b[k] = east * i
            last_w[d, k] = inv[d, k] if prod is None else inv[d, k] * prod
            prod = wi[d, k] if prod is None else wi[d, k] * prod
        prod = None
        for k in range(N):
            first_w[d, k] = tmp_a[k] if prod is None else tmp_a[k] * prod
            prod = tmp_b[k] if prod is None else tmp_b[k] * prod

    def to_solvers(d, send, recv, kind):
        ax = axes[d]
        for s in range(SOLVERS):
            copy = pltpu.make_async_remote_copy(
                send.at[d, s], recv.at[d, ax["me"]], net_sem.at[d, kind, 0], net_sem.at[d, kind, 1],
                device_id=ax["device"](ax["solver"](s)), device_id_type=MESH,
            )
            pl.when(ax["me"] != ax["solver"](s))(copy.start)

            @pl.when(ax["me"] == ax["solver"](s))
            def _():
                recv[d, ax["me"]] = send[d, s]

    def wait_slots(ref, count, sem):
        pltpu.make_async_copy(ref.at[pl.ds(0, count)], ref.at[pl.ds(0, count)], sem).wait()

    def sent_to_solvers(d, send, kind):
        pl.when(axes[d]["solves"])(
            lambda: wait_slots(send.at[d], SOLVERS - 1, net_sem.at[d, kind, 0])
        )
        pl.when(jnp.logical_not(axes[d]["solves"]))(
            lambda: wait_slots(send.at[d], SOLVERS, net_sem.at[d, kind, 0])
        )

    def solver_factor(d):
        @pl.when(axes[d]["solves"])
        def _():
            wait_slots(coef_recv.at[d], N - 1, net_sem.at[d, 0, 1])
            beta = None
            for i in range(N):
                q0, t0, q1, t1 = (coef_recv[d, i, v] for v in range(4))
                if beta is None:
                    dinv = jnp.ones_like(q0)
                    b = jnp.zeros_like(q0)
                    tau = t0
                    beta = t1
                    a = b
                    dq = b
                else:
                    dinv = 1.0 / (1.0 - q0 * beta)
                    b = q1 * beta * dinv
                    tau = t0 * dinv
                    beta = t1 + b * t0
                    a = q1 + b * q0
                    dq = dinv * q0
                for n, value in enumerate((dinv, dq, a, b, tau, beta)):
                    lu[d, i, n] = value

    def solver_solve(d):
        ax = axes[d]

        @pl.when(ax["solves"])
        def _():
            wait_slots(side_recv.at[d], N - 1, net_sem.at[d, 1, 1])
            alpha, alphas, phis = None, [], []
            for i in range(N):
                p0, p1 = side_recv[d, i, 0], side_recv[d, i, 1]
                if alpha is None:
                    phi, alpha = p0, p1
                else:
                    phi = lu[d, i, 0] * p0 + lu[d, i, 1] * alpha
                    alpha = (p1 + lu[d, i, 3] * p0) + lu[d, i, 2] * alpha
                alphas.append(alpha)
                phis.append(phi)
            zero = jnp.zeros((8, LANES), F32)
            first, firsts, lasts = zero, [None] * N, [None] * N
            for i in range(N - 1, -1, -1):
                lasts[i] = alphas[i] + lu[d, i, 5] * first
                first = phis[i] + lu[d, i, 4] * first
                firsts[i] = first
            for i in range(N):
                back_send[d, i, 0] = lasts[i - 1] if i > 0 else zero
                back_send[d, i, 1] = firsts[i + 1] if i < N - 1 else zero

            @pl.loop(0, N)
            def _(i):
                copy = pltpu.make_async_remote_copy(
                    back_send.at[d, i], back_recv.at[d, ax["tile"]],
                    net_sem.at[d, 2, 0], net_sem.at[d, 2, 1],
                    device_id=ax["device"](i), device_id_type=MESH,
                )
                pl.when(i != ax["me"])(copy.start)

            back_recv[d, ax["tile"]] = back_send[d, ax["me"]]

    def wait_back(d):
        pl.when(axes[d]["solves"])(
            lambda: wait_slots(back_recv.at[d], SOLVERS - 1, net_sem.at[d, 2, 1])
        )
        pl.when(jnp.logical_not(axes[d]["solves"]))(
            lambda: wait_slots(back_recv.at[d], SOLVERS, net_sem.at[d, 2, 1])
        )
        return tuple(
            back_recv[d, :, v].reshape(2, N, LANES) for v in range(2)
        )

    def ends_of(d, rhs):
        sums = [None, None]
        for k in range(N):
            b = rhs(k)
            terms = first_w[d, k] * b, last_w[d, k] * b
            sums = [x if s is None else s + x for s, x in zip(sums, terms)]
        for v in range(2):
            for s in range(SOLVERS):
                side_send[d, s, v] = sums[v][s // 2, 8 * (s % 2) : 8 * (s % 2) + 8]

    def particular(d, rhs):
        g = None
        for k in range(N):
            g = inv[d, k] * rhs(k) + (0.0 if g is None else wi[d, k] * g)
            tmp_a[k] = g
        value = g
        part[d, N - 1] = value
        for k in range(N - 2, -1, -1):
            value = tmp_a[k] + ratio_c[d, k] * value
            part[d, k] = value

    loads[2].wait()
    loads[3].wait()
    factor(0, along, cfl_x)

    pl.semaphore_wait(barrier, expected)

    z_copy = [
        pltpu.make_async_remote_copy(
            z_send.at[n], z_face.at[n], z_sem.at[n, 0], z_sem.at[n, 1],
            device_id=(gx, gy, 1 - gz), device_id_type=MESH,
        )
        for n in range(2)
    ]
    y_up = pltpu.make_async_remote_copy(
        y_send.at[1], y_face.at[0], y_sem.at[0, 0], y_sem.at[0, 1],
        device_id=(gx, gy + 1, gz), device_id_type=MESH,
    )
    y_down = pltpu.make_async_remote_copy(
        y_send.at[0], y_face.at[1], y_sem.at[1, 0], y_sem.at[1, 1],
        device_id=(gx, gy - 1, gz), device_id_type=MESH,
    )
    z_copy[0].start()
    pl.when(gy < N - 1)(y_up.start)
    pl.when(gy > 0)(y_down.start)
    to_solvers(0, coef_send, coef_recv, 0)

    weights(0, along, cfl_x)

    for n in range(4, 8):
        loads[n].wait()
    toward = jnp.where(gz == 0, -0.5, 0.5).astype(F32)

    def vertical(v, y):
        mixed = ratio * pair(mix_z, across(y))
        cfl = pair(cfl_z, across(y))
        up = jnp.where(lane == LANES - 1, 0.0, pltpu.roll(v, LANES - 1, 2))
        down = jnp.where(lane == 0, 0.0, pltpu.roll(v, 1, 2))
        return (mixed - 0.5 * cfl) * (up - v) + (mixed + 0.5 * cfl) * (down - v)

    edge_coef = [None, None]
    for y in range(N):
        here = fields[:, across(y), :]
        mixed = ratio * pair(mix, across(y))
        speed = 0.5 * pair(cfl_y, across(y))
        east, west = mixed - speed, mixed + speed
        ahead = fields[:, across(y + 1), :] - here if y < N - 1 else -here
        behind = fields[:, across(y - 1), :] - here if y > 0 else -here
        value = here + (east * ahead + west * behind) + vertical(here, y)
        value = value + weight * pair(load, across(y))
        side[:, along(y), :] = value
        outward = ratio * pair(mix_z, across(y)) + toward * pair(cfl_z, across(y))
        mask_z[y] = jnp.where(lane == face, outward, 0.0)
        if y == 0:
            edge_coef[0] = west
        if y == N - 1:
            edge_coef[1] = east

    factor(1, across, cfl_y)
    to_solvers(1, coef_send, coef_recv, 0)
    weights(1, across, cfl_y)

    z_copy[0].wait_recv()
    pl.when(gy > 0)(y_up.wait_recv)
    pl.when(gy < N - 1)(y_down.wait_recv)
    got = z_face[0]
    for y in range(N):
        value = side[:, along(y), :] + mask_z[y] * unpack_column(got, y)
        if y == 0:
            value = value + edge_coef[0] * y_face[0]
        if y == N - 1:
            value = value + edge_coef[1] * y_face[1]
        side[:, along(y), :] = value

    def first_rhs(k):
        return side[:, across(k), :]

    ends_of(0, first_rhs)
    to_solvers(0, side_send, side_recv, 1)
    solver_factor(0)
    solver_solve(0)
    particular(0, first_rhs)
    left, right = wait_back(0)
    for k in range(N):
        half[:, along(k), :] = part[0, k] + from_left[0, k] * left + from_right[0, k] * right

    packed = jnp.zeros((N, LANES), F32)
    for y in range(N):
        packed = pack_column(half[:, across(y), :], y, packed)
    z_send[1] = packed
    z_copy[1].start()
    for y in range(N):
        here = half[:, across(y), :]
        value = 2.0 * here - side[:, along(y), :] + vertical(here, y)
        side[:, along(y), :] = value + weight * pair(load, across(y))
    solver_factor(1)
    z_copy[1].wait_recv()
    got = z_face[1]
    for y in range(N):
        side[:, along(y), :] = side[:, along(y), :] + mask_z[y] * unpack_column(got, y)

    def second_rhs(k):
        return side[:, along(k), :]

    ends_of(1, second_rhs)
    to_solvers(1, side_send, side_recv, 1)
    solver_solve(1)
    particular(1, second_rhs)
    left, right = wait_back(1)
    for k in range(N):
        result[:, across(k), :] = part[1, k] + from_left[1, k] * left + from_right[1, k] * right
    outs = [
        pltpu.make_async_copy(result.at[f], out, out_sem.at[f]) for f, out in enumerate((t_out, h_out))
    ]
    for copy in outs:
        copy.start()

    for n in range(2):
        z_copy[n].wait_send()
    pl.when(gy < N - 1)(y_up.wait_send)
    pl.when(gy > 0)(y_down.wait_send)
    for d in range(2):
        sent_to_solvers(d, coef_send, 0)
        sent_to_solvers(d, side_send, 1)
        pl.when(axes[d]["solves"])(
            lambda d=d: wait_slots(back_send.at[d], N - 1, net_sem.at[d, 2, 0])
        )
    for copy in outs:
        copy.wait()


def body(*args):
    flat = [a.reshape(N * N, LANES) for a in args]
    block = (N * N, LANES)
    rows = (N, 2, N, LANES)
    both = (2, N, 2, N, LANES)
    vmem = lambda *shape: pltpu.VMEM(shape, F32)
    outs = pl.pallas_call(
        kernel,
        out_shape=[jax.ShapeDtypeStruct(block, F32)] * 2,
        in_specs=[pl.BlockSpec(memory_space=pl.ANY)] * 8,
        out_specs=[pl.BlockSpec(memory_space=pl.ANY)] * 2,
        scratch_shapes=[
            vmem(2, *block),
            *[vmem(*block)] * 6,
            vmem(2, *block),
            vmem(2, *block), vmem(*rows), vmem(2, *block),
            *[vmem(*both)] * 8,
            vmem(*rows), vmem(*rows),
            vmem(2, 2, N, LANES), vmem(2, 2, N, LANES),
            vmem(2, N, LANES), vmem(2, N, LANES),
            vmem(2, SOLVERS, 4, 8, LANES), vmem(2, N, 4, 8, LANES),
            vmem(2, SOLVERS, 2, 8, LANES), vmem(2, N, 2, 8, LANES),
            vmem(2, N, 2, 8, LANES), vmem(2, SOLVERS, 2, 8, LANES),
            vmem(2, N, 6, 8, LANES),
            pltpu.SemaphoreType.DMA((8,)), pltpu.SemaphoreType.DMA((2,)),
            pltpu.SemaphoreType.DMA((2, 2)), pltpu.SemaphoreType.DMA((2, 2)),
            pltpu.SemaphoreType.DMA((2, 3, 2)),
        ],
        compiler_params=pltpu.CompilerParams(
            collective_id=0, has_side_effects=True, vmem_limit_bytes=32 * 1024 * 1024
        ),
    )(*flat)
    return tuple(o.reshape(N, N, LANES) for o in outs)


def solution(mesh):
    spec = P("gx", "gy", "gz")
    return jax.shard_map(
        body, mesh=mesh, in_specs=(spec,) * 8, out_specs=(spec,) * 2, check_vma=False
    )
```

time: 233 us -> 55.8 us (0.24)
  Pallas kernels: 0 us -> 46.4 us
  starting transfers between devices: 46 us -> 0 us
  loops' own time: 44.2 us -> 0 us
  waiting for transfers between devices: 40.8 us -> 0 us
  local copies, waits for them, and re-layouts: 44.7 us -> 8.54 us
  blocking collectives: 36.1 us -> 0 us
  other arithmetic: 19 us -> 0 us
    pallas_call x0 -> x1, Pallas kernels: none -> 46.4 us  [body(): pl.pallas_call(kernel, out_shape=[jax.ShapeDtypeStruct(block, F32)] * 2,...]
    another operation x4 -> x0, loops' own time: 44.2 us -> none  [the longest x2 27.5 us: eliminate(): lax.scan(forward, (upper_in, right_in), (lower_band, diagonal_band, upper...]
    all_to_all x2 -> x0, waiting for transfers between devices: 38.3 us -> none  [the longest x1 29.6 us: body(): lax.all_to_all(packed_y, 'gy', split_axis=1, concat_axis=2, tiled=True)]
    all_to_all x2 -> x0, blocking collectives: 36.1 us -> none  [the longest x1 25.5 us: body(): lax.all_to_all(jnp.moveaxis(solved_y, 0, 2), 'gy', split_axis=2, concat_a...]
    ppermute x8 -> x0, starting transfers between devices: 25.2 us -> none  [the longest x4 19.4 us: extended(): lax.ppermute(last, axis, up)]
    dynamic_slice x2304 -> x0, local copies, waits for them, and re-layouts: 21.2 us -> none  [eliminate(): lax.scan(forward, (upper_in, right_in), (lower_band, diagonal_band, upper...]
    all_to_all x2 -> x0, starting transfers between devices: 20.8 us -> none  [the longest x1 11.8 us: body(): lax.all_to_all(packed_y, 'gy', split_axis=1, concat_axis=2, tiled=True)]
    dynamic_update_slice x1024 -> x0, local copies, waits for them, and re-layouts: 14.6 us -> none  [eliminate(): lax.scan(forward, (upper_in, right_in), (lower_band, diagonal_band, upper...]
where the time goes in v1:
time: 55.8 us; the launch traced here: 55.5 us
  Pallas kernels  46.4 us (83%)
  local copies, waits for them, and re-layouts  8.54 us (15%)
  between operations  0.66 us (1%)
    pallas_call x1, Pallas kernels, body(): pl.pallas_call(kernel, out_shape=[jax.ShapeDtypeStruct(block, F32)] * 2,...  46.4 us
    unnamed x18, local copies, waits for them, and re-layouts  8.54 us

profile of v1, /device:TPU:24, one launch (start us, length us, event | category | flops | bytes accessed | tf_op | source)
XLA Modules:
  0.0 55.5 jit_solution(13245294304216702099)
XLA Ops:
  0.6 0.0 copy-start
  0.6 0.9 %copy-done = f32[16,16,128]{2,1,0:T(8,128)S(1)} copy-done((f32[16,16,128]{2,1,0:T(8,128)S(1)}, f32[16,16,128]{2,1,0:T(8,128)}, u32[]{:S(2)}) %copy-start) | copy-done | bytes 131096
  1.5 0.0 copy-start.1
  1.5 0.9 %copy-done.1 = f32[16,16,128]{2,1,0:T(8,128)S(1)} copy-done((f32[16,16,128]{2,1,0:T(8,128)S(1)}, f32[16,16,128]{2,1,0:T(8,128)}, u32[]{:S(2)}) %copy-start.1) | copy-done | bytes 131096
  2.4 0.0 copy-start.2
  2.4 0.9 %copy-done.2 = f32[16,16,128]{2,1,0:T(8,128)S(1)} copy-done((f32[16,16,128]{2,1,0:T(8,128)S(1)}, f32[16,16,128]{2,1,0:T(8,128)}, u32[]{:S(2)}) %copy-start.2) | copy-done | bytes 131096
  3.3 0.0 copy-start.3
  3.3 0.9 %copy-done.3 = f32[16,16,128]{2,1,0:T(8,128)S(1)} copy-done((f32[16,16,128]{2,1,0:T(8,128)S(1)}, f32[16,16,128]{2,1,0:T(8,128)}, u32[]{:S(2)}) %copy-start.3) | copy-done | bytes 131096
  4.3 0.0 copy-start.4
  4.3 0.9 %copy-done.4 = f32[16,16,128]{2,1,0:T(8,128)S(1)} copy-done((f32[16,16,128]{2,1,0:T(8,128)S(1)}, f32[16,16,128]{2,1,0:T(8,128)}, u32[]{:S(2)}) %copy-start.4) | copy-done | bytes 131096
  5.2 0.0 copy-start.5
  5.2 0.9 %copy-done.5 = f32[16,16,128]{2,1,0:T(8,128)S(1)} copy-done((f32[16,16,128]{2,1,0:T(8,128)S(1)}, f32[16,16,128]{2,1,0:T(8,128)}, u32[]{:S(2)}) %copy-start.5) | copy-done | bytes 131096
  6.1 0.0 copy-start.6
  6.1 0.9 %copy-done.6 = f32[16,16,128]{2,1,0:T(8,128)S(1)} copy-done((f32[16,16,128]{2,1,0:T(8,128)S(1)}, f32[16,16,128]{2,1,0:T(8,128)}, u32[]{:S(2)}) %copy-start.6) | copy-done | bytes 131096
  7.0 0.0 copy-start.7
  7.0 0.9 %copy-done.7 = f32[16,16,128]{2,1,0:T(8,128)S(1)} copy-done((f32[16,16,128]{2,1,0:T(8,128)S(1)}, f32[16,16,128]{2,1,0:T(8,128)}, u32[]{:S(2)}) %copy-start.7) | copy-done | bytes 131096
  7.9 46.4 %shard_map.95 = (f32[256,128]{1,0:T(8,128)S(1)}, f32[256,128]{1,0:T(8,128)S(1)}) custom-call(f32[256,128]{1,0:T(8,128)S(1)} %bitcast.12, f32[256,128]{1,0:T(8,128)S(1)} %bitcast.13, f32[256,128]{1,0:T(8,128)S(1)} %bitcast.14, f32[256,128]{1,0:T(8,128)S(1)} %bitcast.15, f32[256,128]{1,0:T(8,128)S(1)} %bitcast.16, f32[256,128]{1,0:T(8,128)S(1)} %bitcast.17, ...), custom_call_target="tpu_custom_call" | custom-call | tf_op jit(solution)/shard_map/pallas_call | solution.py:427
  54.2 0.7 %copy.12 = f32[16,16,128]{2,1,0:T(8,128)} copy(f32[16,16,128]{2,1,0:T(8,128)S(1)} %bitcast.11) | data formatting | bytes 262144
  54.9 0.7 %copy.13 = f32[16,16,128]{2,1,0:T(8,128)} copy(f32[16,16,128]{2,1,0:T(8,128)S(1)} %bitcast.10) | data formatting | bytes 262144
Async XLA Ops:
  0.6 0.9 %copy-start = (f32[16,16,128]{2,1,0:T(8,128)S(1)}, f32[16,16,128]{2,1,0:T(8,128)}, u32[]{:S(2)}) copy-start(f32[16,16,128]{2,1,0:T(8,128)} %param.8) | copy-start | bytes 393220
  1.5 0.9 %copy-start.1 = (f32[16,16,128]{2,1,0:T(8,128)S(1)}, f32[16,16,128]{2,1,0:T(8,128)}, u32[]{:S(2)}) copy-start(f32[16,16,128]{2,1,0:T(8,128)} %param.9) | copy-start | bytes 393220
  2.4 0.9 %copy-start.2 = (f32[16,16,128]{2,1,0:T(8,128)S(1)}, f32[16,16,128]{2,1,0:T(8,128)}, u32[]{:S(2)}) copy-start(f32[16,16,128]{2,1,0:T(8,128)} %param.10) | copy-start | bytes 393220
  3.3 0.9 %copy-start.3 = (f32[16,16,128]{2,1,0:T(8,128)S(1)}, f32[16,16,128]{2,1,0:T(8,128)}, u32[]{:S(2)}) copy-start(f32[16,16,128]{2,1,0:T(8,128)} %param.11) | copy-start | bytes 393220
  4.3 0.9 %copy-start.4 = (f32[16,16,128]{2,1,0:T(8,128)S(1)}, f32[16,16,128]{2,1,0:T(8,128)}, u32[]{:S(2)}) copy-start(f32[16,16,128]{2,1,0:T(8,128)} %param.12) | copy-start | bytes 393220
  5.2 0.9 %copy-start.5 = (f32[16,16,128]{2,1,0:T(8,128)S(1)}, f32[16,16,128]{2,1,0:T(8,128)}, u32[]{:S(2)}) copy-start(f32[16,16,128]{2,1,0:T(8,128)} %param.13) | copy-start | bytes 393220
  6.1 0.9 %copy-start.6 = (f32[16,16,128]{2,1,0:T(8,128)S(1)}, f32[16,16,128]{2,1,0:T(8,128)}, u32[]{:S(2)}) copy-start(f32[16,16,128]{2,1,0:T(8,128)} %param.14) | copy-start | bytes 393220
  7.0 0.9 %copy-start.7 = (f32[16,16,128]{2,1,0:T(8,128)S(1)}, f32[16,16,128]{2,1,0:T(8,128)}, u32[]{:S(2)}) copy-start(f32[16,16,128]{2,1,0:T(8,128)} %param.15) | copy-start | bytes 393220

commit v2 on v1

--- a/solution.py
+++ b/solution.py
@@ -18,63 +18,70 @@
 def kernel(
     t_in, h_in, load_in, k_in, kz_in, cx_in, cy_in, cz_in,
     t_out, h_out,
-    fields, load, mix, mix_z, cfl_x, cfl_y, cfl_z, result,
+    fields, load, mix, mix_z, cfl_x, cfl_y, cfl_z,
     side, mask_z, half,
     first_w, last_w, inv, wi, ratio_c, from_left, from_right, part,
     tmp_a, tmp_b,
     y_send, y_face, z_send, z_face,
     coef_send, coef_recv, side_send, side_recv, back_send, back_recv, lu,
-    in_sem, out_sem, y_sem, z_sem, net_sem,
+    in_sem, y_sem, z_sem, net_sem, far_sem,
 ):
     gx, gy, gz = lax.axis_index("gx"), lax.axis_index("gy"), lax.axis_index("gz")
     core = lax.rem(gx, 2)
 
     tile_x = lax.rem(lax.div(gx, 2), 4)
-    tile_y = lax.div(gy, 4)
+    tile_y = lax.rem(lax.div(gy, 2), 4)
     axes = (
         dict(
             me=gx, tile=tile_x, solves=gx == 8 * lax.rem(tile_x, 2) + 2 * tile_x,
-            solver=lambda s: 8 * (s % 2) + 2 * s, device=lambda i: (i, gy, gz),
+            solvers=lambda s: (8 * (s % 2) + 2 * s,), device=lambda i: (i, gy, gz),
+            served=N, serve=lambda i: i,
         ),
         dict(
-            me=gy, tile=tile_y, solves=gy == 4 * tile_y + 2 * core,
-            solver=lambda s: 4 * s + 2 * core, device=lambda i: (gx, i, gz),
+            me=gy, tile=tile_y, solves=lax.rem(gy, 2) == core,
+            solvers=lambda s: (2 * s + core, N // 2 + 2 * s + core), device=lambda i: (gx, i, gz),
+            served=N // 2, serve=lambda i: lax.rem(gy + N - N // 4 + i, N),
         ),
     )
-
-    barrier = pltpu.get_barrier_semaphore()
-
-    def greet(device):
-        pl.semaphore_signal(barrier, inc=1, device_id=device, device_id_type=MESH)
-
-    greet((gx, gy, 1 - gz))
-    expected = 1
-    pl.when(gy > 0)(lambda: greet((gx, gy - 1, gz)))
-    pl.when(gy < N - 1)(lambda: greet((gx, gy + 1, gz)))
-    expected += jnp.where(gy > 0, 1, 0) + jnp.where(gy < N - 1, 1, 0)
-    for ax in axes:
-        for s in range(SOLVERS):
-            pl.when(ax["me"] != ax["solver"](s))(
-                functools.partial(greet, ax["device"](ax["solver"](s)))
-            )
-
-        @pl.when(ax["solves"])
-        def _(ax=ax):
-            @pl.loop(0, N)
-            def _(i):
-                pl.when(i != ax["me"])(lambda: greet(ax["device"](i)))
-
-        expected += jnp.where(ax["solves"], N - 1 + SOLVERS - 1, SOLVERS)
 
     loads = [
         pltpu.make_async_copy(src, dst, in_sem.at[n])
         for n, (src, dst) in enumerate((
-            (t_in, fields.at[0]), (h_in, fields.at[1]), (k_in, mix), (cx_in, cfl_x),
+            (k_in, mix), (cx_in, cfl_x), (t_in, fields.at[0]), (h_in, fields.at[1]),
             (cy_in, cfl_y), (kz_in, mix_z), (cz_in, cfl_z), (load_in, load),
         ))
     ]
     for copy in loads:
         copy.start()
+
+    def ring(step):
+        return (gx, lax.rem(gy + step + N, N), gz)
+
+    def signal(sem, device):
+        pl.semaphore_signal(sem, inc=1, device_id=device, device_id_type=MESH)
+
+    barrier = pltpu.get_barrier_semaphore()
+    signal(barrier, (gx, gy, 1 - gz))
+    signal(barrier, ring(1))
+    signal(barrier, ring(-1))
+    for s in range(SOLVERS):
+        (solver,) = axes[0]["solvers"](s)
+        pl.when(gx != solver)(functools.partial(signal, barrier, axes[0]["device"](solver)))
+
+    @pl.when(axes[0]["solves"])
+    def _():
+        @pl.loop(0, N)
+        def _(i):
+            pl.when(i != gx)(lambda: signal(barrier, axes[0]["device"](i)))
+
+    expected = 3 + jnp.where(axes[0]["solves"], N - 1 + SOLVERS - 1, SOLVERS)
+
+    def tell(r):
+        signal(far_sem.at[r], ring(1 << r))
+        signal(far_sem.at[r], ring(-(1 << r)))
+
+    def hear(r):
+        pl.semaphore_wait(far_sem.at[r], 2)
 
     lane = lax.broadcasted_iota(jnp.int32, (2, N, LANES), 2)
     field = lax.broadcasted_iota(jnp.int32, (2, N, LANES), 0)
@@ -103,17 +110,6 @@
         return jnp.stack(
             [pltpu.roll(packed, LANES - 1 - (1 + N * f + y) + gz, 1) for f in range(2)]
         )
-
-    loads[0].wait()
-    loads[1].wait()
-    y_send[0] = fields[:, across(0), :]
-    y_send[1] = fields[:, across(N - 1), :]
-    packed = jnp.zeros((N, LANES), F32)
-    for y in range(N):
-        packed = pack_column(fields[:, across(y), :], y, packed)
-    z_send[0] = packed
-    pl.when(gy == 0)(lambda: y_face.__setitem__(0, jnp.zeros((2, N, LANES), F32)))
-    pl.when(gy == N - 1)(lambda: y_face.__setitem__(1, jnp.zeros((2, N, LANES), F32)))
 
     def factor(d, rows, cfl):
         def bands(k):
@@ -174,20 +170,24 @@
     def to_solvers(d, send, recv, kind):
         ax = axes[d]
         for s in range(SOLVERS):
-            copy = pltpu.make_async_remote_copy(
-                send.at[d, s], recv.at[d, ax["me"]], net_sem.at[d, kind, 0], net_sem.at[d, kind, 1],
-                device_id=ax["device"](ax["solver"](s)), device_id_type=MESH,
-            )
-            pl.when(ax["me"] != ax["solver"](s))(copy.start)
-
-            @pl.when(ax["me"] == ax["solver"](s))
-            def _():
-                recv[d, ax["me"]] = send[d, s]
+            for solver in ax["solvers"](s):
+                copy = pltpu.make_async_remote_copy(
+                    send.at[d, s], recv.at[d, ax["me"]],
+                    net_sem.at[d, kind, 0], net_sem.at[d, kind, 1],
+                    device_id=ax["device"](solver), device_id_type=MESH,
+                )
+                pl.when(ax["me"] != solver)(copy.start)
+
+                @pl.when(ax["me"] == solver)
+                def _():
+                    recv[d, ax["me"]] = send[d, s]
 
     def wait_slots(ref, count, sem):
         pltpu.make_async_copy(ref.at[pl.ds(0, count)], ref.at[pl.ds(0, count)], sem).wait()
 
     def sent_to_solvers(d, send, kind):
+        for _ in axes[d]["solvers"](0)[1:]:
+            wait_slots(send.at[d], SOLVERS, net_sem.at[d, kind, 0])
         pl.when(axes[d]["solves"])(
             lambda: wait_slots(send.at[d], SOLVERS - 1, net_sem.at[d, kind, 0])
         )
@@ -245,14 +245,15 @@
                 back_send[d, i, 0] = lasts[i - 1] if i > 0 else zero
                 back_send[d, i, 1] = firsts[i + 1] if i < N - 1 else zero
 
-            @pl.loop(0, N)
+            @pl.loop(0, ax["served"])
             def _(i):
+                j = ax["serve"](i)
                 copy = pltpu.make_async_remote_copy(
-                    back_send.at[d, i], back_recv.at[d, ax["tile"]],
+                    back_send.at[d, j], back_recv.at[d, ax["tile"]],
                     net_sem.at[d, 2, 0], net_sem.at[d, 2, 1],
-                    device_id=ax["device"](i), device_id_type=MESH,
+                    device_id=ax["device"](j), device_id_type=MESH,
                 )
-                pl.when(i != ax["me"])(copy.start)
+                pl.when(j != ax["me"])(copy.start)
 
             back_recv[d, ax["tile"]] = back_send[d, ax["me"]]
 
@@ -288,9 +289,20 @@
             value = tmp_a[k] + ratio_c[d, k] * value
             part[d, k] = value
 
+    loads[0].wait()
+    loads[1].wait()
+    factor(0, along, cfl_x)
+
     loads[2].wait()
     loads[3].wait()
-    factor(0, along, cfl_x)
+    y_send[0] = fields[:, across(0), :]
+    y_send[1] = fields[:, across(N - 1), :]
+    packed = jnp.zeros((N, LANES), F32)
+    for y in range(N):
+        packed = pack_column(fields[:, across(y), :], y, packed)
+    z_send[0] = packed
+    pl.when(gy == 0)(lambda: y_face.__setitem__(0, jnp.zeros((2, N, LANES), F32)))
+    pl.when(gy == N - 1)(lambda: y_face.__setitem__(1, jnp.zeros((2, N, LANES), F32)))
 
     pl.semaphore_wait(barrier, expected)
 
@@ -313,6 +325,7 @@
     pl.when(gy < N - 1)(y_up.start)
     pl.when(gy > 0)(y_down.start)
     to_solvers(0, coef_send, coef_recv, 0)
+    tell(0)
 
     weights(0, along, cfl_x)
 
@@ -346,8 +359,9 @@
             edge_coef[1] = east
 
     factor(1, across, cfl_y)
-    to_solvers(1, coef_send, coef_recv, 0)
     weights(1, across, cfl_y)
+    hear(0)
+    tell(1)
 
     z_copy[0].wait_recv()
     pl.when(gy > 0)(y_up.wait_recv)
@@ -366,9 +380,13 @@
 
     ends_of(0, first_rhs)
     to_solvers(0, side_send, side_recv, 1)
+    hear(1)
+    tell(2)
     solver_factor(0)
     solver_solve(0)
     particular(0, first_rhs)
+    hear(2)
+    to_solvers(1, coef_send, coef_recv, 0)
     left, right = wait_back(0)
     for k in range(N):
         half[:, along(k), :] = part[0, k] + from_left[0, k] * left + from_right[0, k] * right
@@ -382,7 +400,6 @@
         here = half[:, across(y), :]
         value = 2.0 * here - side[:, along(y), :] + vertical(here, y)
         side[:, along(y), :] = value + weight * pair(load, across(y))
-    solver_factor(1)
     z_copy[1].wait_recv()
     got = z_face[1]
     for y in range(N):
@@ -393,16 +410,14 @@
 
     ends_of(1, second_rhs)
     to_solvers(1, side_send, side_recv, 1)
+    solver_factor(1)
     solver_solve(1)
     particular(1, second_rhs)
     left, right = wait_back(1)
     for k in range(N):
-        result[:, across(k), :] = part[1, k] + from_left[1, k] * left + from_right[1, k] * right
-    outs = [
-        pltpu.make_async_copy(result.at[f], out, out_sem.at[f]) for f, out in enumerate((t_out, h_out))
-    ]
-    for copy in outs:
-        copy.start()
+        value = part[1, k] + from_left[1, k] * left + from_right[1, k] * right
+        t_out[across(k), :] = value[0]
+        h_out[across(k), :] = value[1]
 
     for n in range(2):
         z_copy[n].wait_send()
@@ -412,10 +427,8 @@
         sent_to_solvers(d, coef_send, 0)
         sent_to_solvers(d, side_send, 1)
         pl.when(axes[d]["solves"])(
-            lambda d=d: wait_slots(back_send.at[d], N - 1, net_sem.at[d, 2, 0])
-        )
-    for copy in outs:
-        copy.wait()
+            lambda d=d: wait_slots(back_send.at[d], axes[d]["served"] - 1, net_sem.at[d, 2, 0])
+        )
 
 
 def body(*args):
@@ -427,12 +440,11 @@
     outs = pl.pallas_call(
         kernel,
         out_shape=[jax.ShapeDtypeStruct(block, F32)] * 2,
-        in_specs=[pl.BlockSpec(memory_space=pl.ANY)] * 8,
-        out_specs=[pl.BlockSpec(memory_space=pl.ANY)] * 2,
+        in_specs=[pl.BlockSpec(memory_space=pltpu.HBM)] * 8,
+        out_specs=[pl.BlockSpec(memory_space=pltpu.VMEM)] * 2,
         scratch_shapes=[
             vmem(2, *block),
             *[vmem(*block)] * 6,
-            vmem(2, *block),
             vmem(2, *block), vmem(*rows), vmem(2, *block),
             *[vmem(*both)] * 8,
             vmem(*rows), vmem(*rows),
@@ -442,12 +454,12 @@
             vmem(2, SOLVERS, 2, 8, LANES), vmem(2, N, 2, 8, LANES),
             vmem(2, N, 2, 8, LANES), vmem(2, SOLVERS, 2, 8, LANES),
             vmem(2, N, 6, 8, LANES),
-            pltpu.SemaphoreType.DMA((8,)), pltpu.SemaphoreType.DMA((2,)),
+            pltpu.SemaphoreType.DMA((8,)),
             pltpu.SemaphoreType.DMA((2, 2)), pltpu.SemaphoreType.DMA((2, 2)),
-            pltpu.SemaphoreType.DMA((2, 3, 2)),
+            pltpu.SemaphoreType.DMA((2, 3, 2)), pltpu.SemaphoreType.REGULAR((3,)),
         ],
         compiler_params=pltpu.CompilerParams(
-            collective_id=0, has_side_effects=True, vmem_limit_bytes=32 * 1024 * 1024
+            collective_id=0, has_side_effects=True, vmem_limit_bytes=56229888
         ),
     )(*flat)
     return tuple(o.reshape(N, N, LANES) for o in outs)

time: 55.8 us -> 43.3 us (0.78)
  the two profiles are of different devices: /device:TPU:24 before, /device:TPU:8 now
where the time goes in v2:
time: 43.3 us; the launch traced here: 43.2 us
  Pallas kernels  41.2 us (95%)
  local copies, waits for them, and re-layouts  1.31 us (3%)
  between operations  0.64 us (1%)
    pallas_call x1, Pallas kernels, body(): pl.pallas_call(kernel, out_shape=[jax.ShapeDtypeStruct(block, F32)] * 2,...  41.2 us
    unnamed x2, local copies, waits for them, and re-layouts  1.31 us

profile of v2, /device:TPU:8, one launch (start us, length us, event | category | flops | bytes accessed | tf_op | source)
XLA Modules:
  0.0 43.2 jit_solution(4732010335800811844)
XLA Ops:
  0.6 41.2 %shard_map.95 = (f32[256,128]{1,0:T(8,128)S(1)}, f32[256,128]{1,0:T(8,128)S(1)}) custom-call(f32[256,128]{1,0:T(8,128)} %bitcast.12, f32[256,128]{1,0:T(8,128)} %bitcast.13, f32[256,128]{1,0:T(8,128)} %bitcast.14, f32[256,128]{1,0:T(8,128)} %bitcast.15, f32[256,128]{1,0:T(8,128)} %bitcast.16, f32[256,128]{1,0:T(8,128)} %bitcast.17, f32[256,128]{1,0:T(8,128)} %bitcast.18, ...), custom_call_target="tpu_custom_call" | custom-call | tf_op jit(solution)/shard_map/pallas_call | solution.py:440
  41.9 0.7 %copy.12 = f32[16,16,128]{2,1,0:T(8,128)} copy(f32[16,16,128]{2,1,0:T(8,128)S(1)} %bitcast.11) | data formatting | bytes 262144
  42.5 0.7 %copy.13 = f32[16,16,128]{2,1,0:T(8,128)} copy(f32[16,16,128]{2,1,0:T(8,128)S(1)} %bitcast.10) | data formatting | bytes 262144

commit v3 on v2

--- a/solution.py
+++ b/solution.py
@@ -22,9 +22,9 @@
     side, mask_z, half,
     first_w, last_w, inv, wi, ratio_c, from_left, from_right, part,
     tmp_a, tmp_b,
-    y_send, y_face, z_send, z_face,
+    y_send, y_face, z_send, z_face, pull_send, pull, extra_send, extra,
     coef_send, coef_recv, side_send, side_recv, back_send, back_recv, lu,
-    in_sem, y_sem, z_sem, net_sem, far_sem,
+    in_sem, y_sem, z_sem, net_sem, pull_sem, extra_sem, far_sem,
 ):
     gx, gy, gz = lax.axis_index("gx"), lax.axis_index("gy"), lax.axis_index("gz")
     core = lax.rem(gx, 2)
@@ -225,9 +225,21 @@
         @pl.when(ax["solves"])
         def _():
             wait_slots(side_recv.at[d], N - 1, net_sem.at[d, 1, 1])
+            if d == 1:
+                wait_slots(extra, N, extra_sem.at[1])
+            on_face = lane2[:8] == face
+            start = 2 * N * lax.div(ax["tile"], 2) + 8 * lax.rem(ax["tile"], 2)
+            spot = lane2[:8] - start - lax.broadcasted_iota(jnp.int32, (8, LANES), 0)
             alpha, alphas, phis = None, [], []
             for i in range(N):
                 p0, p1 = side_recv[d, i, 0], side_recv[d, i, 1]
+                if d == 1:
+                    sent = jnp.broadcast_to(extra[i], (8, LANES))
+                    d0, d1 = (
+                        jnp.sum(jnp.where(spot == N * v, sent, 0.0), axis=1, keepdims=True) for v in range(2)
+                    )
+                    p0 = p0 + jnp.where(on_face, d0, 0.0)
+                    p1 = p1 + jnp.where(on_face, d1, 0.0)
                 if alpha is None:
                     phi, alpha = p0, p1
                 else:
@@ -360,6 +372,17 @@
 
     factor(1, across, cfl_y)
     weights(1, across, cfl_y)
+
+    for v, ws in enumerate((first_w, last_w)):
+        packed = jnp.zeros((N, LANES), F32)
+        for y in range(N):
+            packed = pack_column(ws[1, y] * mask_z[y], y, packed)
+        pull_send[v] = packed
+    pull_copy = pltpu.make_async_remote_copy(
+        pull_send, pull, pull_sem.at[0], pull_sem.at[1],
+        device_id=(gx, gy, 1 - gz), device_id_type=MESH,
+    )
+    pull_copy.start()
     hear(0)
     tell(1)
 
@@ -386,6 +409,7 @@
     solver_solve(0)
     particular(0, first_rhs)
     hear(2)
+    signal(far_sem.at[3], (gx, gy, 1 - gz))
     to_solvers(1, coef_send, coef_recv, 0)
     left, right = wait_back(0)
     for k in range(N):
@@ -396,23 +420,42 @@
         packed = pack_column(half[:, across(y), :], y, packed)
     z_send[1] = packed
     z_copy[1].start()
+
+    pull_copy.wait_recv()
+    sums = [pull[v] * packed for v in range(2)]
+    row = lax.broadcasted_iota(jnp.int32, (N, LANES), 0)
+    spread = jnp.zeros((N, LANES), F32)
+    for f in range(2):
+        mine = jnp.logical_and(lane2 > N * f, lane2 <= N * f + N)
+        for v in range(2):
+            total = jnp.sum(jnp.where(mine, sums[v], 0.0), axis=1, keepdims=True)
+            spread = jnp.where(lane2 == N * (2 * f + v) + row, total, spread)
+    extra_send[0] = jnp.sum(spread, axis=0, keepdims=True)
+    pl.semaphore_wait(far_sem.at[3], 1)
+    for s in range(SOLVERS):
+        for solver in axes[1]["solvers"](s):
+            pltpu.make_async_remote_copy(
+                extra_send.at[0], extra.at[gy], extra_sem.at[0], extra_sem.at[1],
+                device_id=(gx, solver, 1 - gz), device_id_type=MESH,
+            ).start()
+
     for y in range(N):
         here = half[:, across(y), :]
         value = 2.0 * here - side[:, along(y), :] + vertical(here, y)
         side[:, along(y), :] = value + weight * pair(load, across(y))
+
+    def second_rhs(k):
+        return side[:, along(k), :]
+
+    ends_of(1, second_rhs)
+    to_solvers(1, side_send, side_recv, 1)
     z_copy[1].wait_recv()
     got = z_face[1]
     for y in range(N):
         side[:, along(y), :] = side[:, along(y), :] + mask_z[y] * unpack_column(got, y)
-
-    def second_rhs(k):
-        return side[:, along(k), :]
-
-    ends_of(1, second_rhs)
-    to_solvers(1, side_send, side_recv, 1)
+    particular(1, second_rhs)
     solver_factor(1)
     solver_solve(1)
-    particular(1, second_rhs)
     left, right = wait_back(1)
     for k in range(N):
         value = part[1, k] + from_left[1, k] * left + from_right[1, k] * right
@@ -421,6 +464,9 @@
 
     for n in range(2):
         z_copy[n].wait_send()
+    for _ in range(2 * SOLVERS):
+        wait_slots(extra_send, 1, extra_sem.at[0])
+    pull_copy.wait_send()
     pl.when(gy < N - 1)(y_up.wait_send)
     pl.when(gy > 0)(y_down.wait_send)
     for d in range(2):
@@ -450,13 +496,16 @@
             vmem(*rows), vmem(*rows),
             vmem(2, 2, N, LANES), vmem(2, 2, N, LANES),
             vmem(2, N, LANES), vmem(2, N, LANES),
+            vmem(2, N, LANES), vmem(2, N, LANES),
+            vmem(1, 1, LANES), vmem(N, 1, LANES),
             vmem(2, SOLVERS, 4, 8, LANES), vmem(2, N, 4, 8, LANES),
             vmem(2, SOLVERS, 2, 8, LANES), vmem(2, N, 2, 8, LANES),
             vmem(2, N, 2, 8, LANES), vmem(2, SOLVERS, 2, 8, LANES),
             vmem(2, N, 6, 8, LANES),
             pltpu.SemaphoreType.DMA((8,)),
             pltpu.SemaphoreType.DMA((2, 2)), pltpu.SemaphoreType.DMA((2, 2)),
-            pltpu.SemaphoreType.DMA((2, 3, 2)), pltpu.SemaphoreType.REGULAR((3,)),
+            pltpu.SemaphoreType.DMA((2, 3, 2)), pltpu.SemaphoreType.DMA((2,)),
+            pltpu.SemaphoreType.DMA((2,)), pltpu.SemaphoreType.REGULAR((4,)),
         ],
         compiler_params=pltpu.CompilerParams(
             collective_id=0, has_side_effects=True, vmem_limit_bytes=56229888

time: 43.3 us -> 41.4 us (0.956)
  the two profiles are of different devices: /device:TPU:8 before, /device:TPU:32 now
where the time goes in v3:
time: 41.4 us; the launch traced here: 41.2 us
  Pallas kernels  39.3 us (95%)
  local copies, waits for them, and re-layouts  1.31 us (3%)
  between operations  0.64 us (2%)
    pallas_call x1, Pallas kernels, body(): pl.pallas_call(kernel, out_shape=[jax.ShapeDtypeStruct(block, F32)] * 2,...  39.3 us
    unnamed x2, local copies, waits for them, and re-layouts  1.31 us

profile of v3, /device:TPU:32, one launch (start us, length us, event | category | flops | bytes accessed | tf_op | source)
XLA Modules:
  0.0 41.2 jit_solution(8240918248701153125)
XLA Ops:
  0.6 39.3 %shard_map.95 = (f32[256,128]{1,0:T(8,128)S(1)}, f32[256,128]{1,0:T(8,128)S(1)}) custom-call(f32[256,128]{1,0:T(8,128)} %bitcast.12, f32[256,128]{1,0:T(8,128)} %bitcast.13, f32[256,128]{1,0:T(8,128)} %bitcast.14, f32[256,128]{1,0:T(8,128)} %bitcast.15, f32[256,128]{1,0:T(8,128)} %bitcast.16, f32[256,128]{1,0:T(8,128)} %bitcast.17, f32[256,128]{1,0:T(8,128)} %bitcast.18, ...), custom_call_target="tpu_custom_call" | custom-call | tf_op jit(solution)/shard_map/pallas_call | solution.py:486
  39.9 0.7 %copy.12 = f32[16,16,128]{2,1,0:T(8,128)} copy(f32[16,16,128]{2,1,0:T(8,128)S(1)} %bitcast.11) | data formatting | bytes 262144
  40.6 0.7 %copy.13 = f32[16,16,128]{2,1,0:T(8,128)} copy(f32[16,16,128]{2,1,0:T(8,128)S(1)} %bitcast.10) | data formatting | bytes 262144

commit v4 on v3

--- a/solution.py
+++ b/solution.py
@@ -29,18 +29,30 @@
     gx, gy, gz = lax.axis_index("gx"), lax.axis_index("gy"), lax.axis_index("gz")
     core = lax.rem(gx, 2)
 
-    tile_x = lax.rem(lax.div(gx, 2), 4)
-    tile_y = lax.rem(lax.div(gy, 2), 4)
+    half_x, chip_x = lax.div(gx, N // 2), lax.rem(lax.div(gx, 2), 4)
+    odd = lax.rem(gy + core, 2)
+
+    def solver_x(other_half, step):
+        chip = lax.rem(chip_x + step, 4)
+        return chip, N // 2 * lax.rem(half_x + other_half, 2) + 2 * chip
+
+    def solver_y(step):
+        j = lax.rem(gy + step - odd + N, N)
+        return lax.rem(lax.div(j, 2), 4), j
+
     axes = (
         dict(
-            me=gx, tile=tile_x, solves=gx == 8 * lax.rem(tile_x, 2) + 2 * tile_x,
-            solvers=lambda s: (8 * (s % 2) + 2 * s,), device=lambda i: (i, gy, gz),
-            served=N, serve=lambda i: i,
+            me=gx, tile=chip_x, solves=core == 0, device=lambda i: (i, gy, gz),
+            solvers=[solver_x(*step) for step in ((1, 2), (1, 1), (1, 3), (0, 2), (1, 0), (0, 1), (0, 3), (0, 0))],
+            served=[
+                N // 2 * half_x + 2 * lax.rem(chip_x + step, 4) + c
+                for step, c in ((2, 1), (2, 0), (1, 1), (3, 1), (1, 0), (3, 0), (0, 1))
+            ],
         ),
         dict(
-            me=gy, tile=tile_y, solves=lax.rem(gy, 2) == core,
-            solvers=lambda s: (2 * s + core, N // 2 + 2 * s + core), device=lambda i: (gx, i, gz),
-            served=N // 2, serve=lambda i: lax.rem(gy + N - N // 4 + i, N),
+            me=gy, tile=lax.rem(lax.div(gy, 2), 4), solves=odd == 0, device=lambda i: (gx, i, gz),
+            solvers=[solver_y(step) for step in (8, -6, 6, -4, 4, -2, 2, 0)],
+            served=[lax.rem(gy + step + N, N) for step in (-4, 3, -3, 2, -2, 1, -1)],
         ),
     )
 
@@ -62,10 +74,9 @@
 
     barrier = pltpu.get_barrier_semaphore()
     signal(barrier, (gx, gy, 1 - gz))
-    signal(barrier, ring(1))
-    signal(barrier, ring(-1))
-    for s in range(SOLVERS):
-        (solver,) = axes[0]["solvers"](s)
+    for step in (1, -1, 2, -2):
+        signal(barrier, ring(step))
+    for _, solver in axes[0]["solvers"]:
         pl.when(gx != solver)(functools.partial(signal, barrier, axes[0]["device"](solver)))
 
     @pl.when(axes[0]["solves"])
@@ -74,11 +85,11 @@
         def _(i):
             pl.when(i != gx)(lambda: signal(barrier, axes[0]["device"](i)))
 
-    expected = 3 + jnp.where(axes[0]["solves"], N - 1 + SOLVERS - 1, SOLVERS)
+    expected = 5 + jnp.where(axes[0]["solves"], N - 1 + 2 * SOLVERS - 1, 2 * SOLVERS)
 
     def tell(r):
-        signal(far_sem.at[r], ring(1 << r))
-        signal(far_sem.at[r], ring(-(1 << r)))
+        signal(far_sem.at[r], ring(2 << r))
+        signal(far_sem.at[r], ring(-(2 << r)))
 
     def hear(r):
         pl.semaphore_wait(far_sem.at[r], 2)
@@ -169,25 +180,23 @@
 
     def to_solvers(d, send, recv, kind):
         ax = axes[d]
-        for s in range(SOLVERS):
-            for solver in ax["solvers"](s):
-                copy = pltpu.make_async_remote_copy(
-                    send.at[d, s], recv.at[d, ax["me"]],
-                    net_sem.at[d, kind, 0], net_sem.at[d, kind, 1],
-                    device_id=ax["device"](solver), device_id_type=MESH,
-                )
-                pl.when(ax["me"] != solver)(copy.start)
-
-                @pl.when(ax["me"] == solver)
-                def _():
-                    recv[d, ax["me"]] = send[d, s]
+        for s, solver in ax["solvers"]:
+            copy = pltpu.make_async_remote_copy(
+                send.at[d, s], recv.at[d, ax["me"]],
+                net_sem.at[d, kind, 0], net_sem.at[d, kind, 1],
+                device_id=ax["device"](solver), device_id_type=MESH,
+            )
+            pl.when(ax["me"] != solver)(copy.start)
+
+        @pl.when(ax["solves"])
+        def _():
+            recv[d, ax["me"]] = send[d, ax["tile"]]
 
     def wait_slots(ref, count, sem):
         pltpu.make_async_copy(ref.at[pl.ds(0, count)], ref.at[pl.ds(0, count)], sem).wait()
 
     def sent_to_solvers(d, send, kind):
-        for _ in axes[d]["solvers"](0)[1:]:
-            wait_slots(send.at[d], SOLVERS, net_sem.at[d, kind, 0])
+        wait_slots(send.at[d], SOLVERS, net_sem.at[d, kind, 0])
         pl.when(axes[d]["solves"])(
             lambda: wait_slots(send.at[d], SOLVERS - 1, net_sem.at[d, kind, 0])
         )
@@ -257,15 +266,12 @@
                 back_send[d, i, 0] = lasts[i - 1] if i > 0 else zero
                 back_send[d, i, 1] = firsts[i + 1] if i < N - 1 else zero
 
-            @pl.loop(0, ax["served"])
-            def _(i):
-                j = ax["serve"](i)
-                copy = pltpu.make_async_remote_copy(
+            for j in ax["served"]:
+                pltpu.make_async_remote_copy(
                     back_send.at[d, j], back_recv.at[d, ax["tile"]],
                     net_sem.at[d, 2, 0], net_sem.at[d, 2, 1],
                     device_id=ax["device"](j), device_id_type=MESH,
-                )
-                pl.when(j != ax["me"])(copy.start)
+                ).start()
 
             back_recv[d, ax["tile"]] = back_send[d, ax["me"]]
 
@@ -403,14 +409,12 @@
 
     ends_of(0, first_rhs)
     to_solvers(0, side_send, side_recv, 1)
+    solver_factor(0)
     hear(1)
-    tell(2)
-    solver_factor(0)
+    signal(far_sem.at[2], (gx, gy, 1 - gz))
+    to_solvers(1, coef_send, coef_recv, 0)
     solver_solve(0)
     particular(0, first_rhs)
-    hear(2)
-    signal(far_sem.at[3], (gx, gy, 1 - gz))
-    to_solvers(1, coef_send, coef_recv, 0)
     left, right = wait_back(0)
     for k in range(N):
         half[:, along(k), :] = part[0, k] + from_left[0, k] * left + from_right[0, k] * right
@@ -431,13 +435,12 @@
             total = jnp.sum(jnp.where(mine, sums[v], 0.0), axis=1, keepdims=True)
             spread = jnp.where(lane2 == N * (2 * f + v) + row, total, spread)
     extra_send[0] = jnp.sum(spread, axis=0, keepdims=True)
-    pl.semaphore_wait(far_sem.at[3], 1)
-    for s in range(SOLVERS):
-        for solver in axes[1]["solvers"](s):
-            pltpu.make_async_remote_copy(
-                extra_send.at[0], extra.at[gy], extra_sem.at[0], extra_sem.at[1],
-                device_id=(gx, solver, 1 - gz), device_id_type=MESH,
-            ).start()
+    pl.semaphore_wait(far_sem.at[2], 1)
+    for _, solver in axes[1]["solvers"]:
+        pltpu.make_async_remote_copy(
+            extra_send.at[0], extra.at[gy], extra_sem.at[0], extra_sem.at[1],
+            device_id=(gx, solver, 1 - gz), device_id_type=MESH,
+        ).start()
 
     for y in range(N):
         here = half[:, across(y), :]
@@ -473,7 +476,7 @@
         sent_to_solvers(d, coef_send, 0)
         sent_to_solvers(d, side_send, 1)
         pl.when(axes[d]["solves"])(
-            lambda d=d: wait_slots(back_send.at[d], axes[d]["served"] - 1, net_sem.at[d, 2, 0])
+            lambda d=d: wait_slots(back_send.at[d], len(axes[d]["served"]), net_sem.at[d, 2, 0])
         )
 
 
@@ -505,7 +508,7 @@
             pltpu.SemaphoreType.DMA((8,)),
             pltpu.SemaphoreType.DMA((2, 2)), pltpu.SemaphoreType.DMA((2, 2)),
             pltpu.SemaphoreType.DMA((2, 3, 2)), pltpu.SemaphoreType.DMA((2,)),
-            pltpu.SemaphoreType.DMA((2,)), pltpu.SemaphoreType.REGULAR((4,)),
+            pltpu.SemaphoreType.DMA((2,)), pltpu.SemaphoreType.REGULAR((3,)),
         ],
         compiler_params=pltpu.CompilerParams(
             collective_id=0, has_side_effects=True, vmem_limit_bytes=56229888

time: 41.4 us -> 40.4 us (0.976)
  the two profiles are of different devices: /device:TPU:32 before, /device:TPU:2 now
where the time goes in v4:
time: 40.4 us; the launch traced here: 40.2 us
  Pallas kernels  38.3 us (95%)
  local copies, waits for them, and re-layouts  1.31 us (3%)
  between operations  0.64 us (2%)
    pallas_call x1, Pallas kernels, body(): pl.pallas_call(kernel, out_shape=[jax.ShapeDtypeStruct(block, F32)] * 2,...  38.3 us
    unnamed x2, local copies, waits for them, and re-layouts  1.31 us

profile of v4, /device:TPU:2, one launch (start us, length us, event | category | flops | bytes accessed | tf_op | source)
XLA Modules:
  0.0 40.2 jit_solution(6548581063468943224)
XLA Ops:
  0.6 38.3 %shard_map.95 = (f32[256,128]{1,0:T(8,128)S(1)}, f32[256,128]{1,0:T(8,128)S(1)}) custom-call(f32[256,128]{1,0:T(8,128)} %bitcast.12, f32[256,128]{1,0:T(8,128)} %bitcast.13, f32[256,128]{1,0:T(8,128)} %bitcast.14, f32[256,128]{1,0:T(8,128)} %bitcast.15, f32[256,128]{1,0:T(8,128)} %bitcast.16, f32[256,128]{1,0:T(8,128)} %bitcast.17, f32[256,128]{1,0:T(8,128)} %bitcast.18, ...), custom_call_target="tpu_custom_call" | custom-call | tf_op jit(solution)/shard_map/pallas_call | solution.py:489
  38.9 0.7 %copy.12 = f32[16,16,128]{2,1,0:T(8,128)} copy(f32[16,16,128]{2,1,0:T(8,128)S(1)} %bitcast.11) | data formatting | bytes 262144
  39.6 0.7 %copy.13 = f32[16,16,128]{2,1,0:T(8,128)} copy(f32[16,16,128]{2,1,0:T(8,128)S(1)} %bitcast.10) | data formatting | bytes 262144

commit v5 on v4

--- a/solution.py
+++ b/solution.py
@@ -17,7 +17,7 @@
 
 def kernel(
     t_in, h_in, load_in, k_in, kz_in, cx_in, cy_in, cz_in,
-    t_out, h_out,
+    t_out, h_out, one_out,
     fields, load, mix, mix_z, cfl_x, cfl_y, cfl_z,
     side, mask_z, half,
     first_w, last_w, inv, wi, ratio_c, from_left, from_right, part,
@@ -52,7 +52,7 @@
         dict(
             me=gy, tile=lax.rem(lax.div(gy, 2), 4), solves=odd == 0, device=lambda i: (gx, i, gz),
             solvers=[solver_y(step) for step in (8, -6, 6, -4, 4, -2, 2, 0)],
-            served=[lax.rem(gy + step + N, N) for step in (-4, 3, -3, 2, -2, 1, -1)],
+            served=[lax.rem(gy + step + N, N) for step in (4, -3, 3, -2, 2, -1, 1)],
         ),
     )
 
@@ -460,6 +460,7 @@
     solver_factor(1)
     solver_solve(1)
     left, right = wait_back(1)
+    one_out[...] = jnp.ones((N, LANES), F32)
     for k in range(N):
         value = part[1, k] + from_left[1, k] * left + from_right[1, k] * right
         t_out[across(k), :] = value[0]
@@ -488,9 +489,9 @@
     vmem = lambda *shape: pltpu.VMEM(shape, F32)
     outs = pl.pallas_call(
         kernel,
-        out_shape=[jax.ShapeDtypeStruct(block, F32)] * 2,
+        out_shape=[jax.ShapeDtypeStruct(block, F32)] * 2 + [jax.ShapeDtypeStruct((N, LANES), F32)],
         in_specs=[pl.BlockSpec(memory_space=pltpu.HBM)] * 8,
-        out_specs=[pl.BlockSpec(memory_space=pltpu.VMEM)] * 2,
+        out_specs=[pl.BlockSpec(memory_space=pltpu.VMEM)] * 3,
         scratch_shapes=[
             vmem(2, *block),
             *[vmem(*block)] * 6,
@@ -514,7 +515,7 @@
             collective_id=0, has_side_effects=True, vmem_limit_bytes=56229888
         ),
     )(*flat)
-    return tuple(o.reshape(N, N, LANES) for o in outs)
+    return tuple(o.reshape(N, N, LANES) * outs[2][None] for o in outs[:2])
 
 
 def solution(mesh):

time: 40.4 us -> 39.9 us (0.988)
  the two profiles are of different devices: /device:TPU:2 before, /device:TPU:1 now
where the time goes in v5:
time: 39.9 us; the launch traced here: 39.8 us
  Pallas kernels  38.4 us (96%)
  other arithmetic  0.72 us (2%)
  between operations  0.64 us (2%)
    pallas_call x1, Pallas kernels, body(): pl.pallas_call(kernel, out_shape=[jax.ShapeDtypeStruct(block, F32)] * 2 +...  38.4 us

profile of v5, /device:TPU:1, one launch (start us, length us, event | category | flops | bytes accessed | tf_op | source)
XLA Modules:
  0.0 39.8 jit_solution(5733716047464603329)
XLA Ops:
  0.6 38.4 %shard_map.95 = (f32[256,128]{1,0:T(8,128)S(1)}, f32[256,128]{1,0:T(8,128)S(1)}, f32[16,128]{1,0:T(8,128)S(1)}) custom-call(f32[256,128]{1,0:T(8,128)} %bitcast.12, f32[256,128]{1,0:T(8,128)} %bitcast.13, f32[256,128]{1,0:T(8,128)} %bitcast.14, f32[256,128]{1,0:T(8,128)} %bitcast.15, f32[256,128]{1,0:T(8,128)} %bitcast.16, f32[256,128]{1,0:T(8,128)} %bitcast.17, ...), custom_call_target="tpu_custom_call" | custom-call | tf_op jit(solution)/shard_map/pallas_call | solution.py:490
  39.1 0.7 %broadcast_multiply_fusion = (f32[16,16,128]{2,1,0:T(8,128)}, f32[16,16,128]{2,1,0:T(8,128)}) fusion(f32[16,16,128]{2,1,0:T(8,128)S(1)} %bitcast.11, f32[16,128]{1,0:T(8,128)S(1)} %get-tuple-element.6, f32[16,16,128]{2,1,0:T(8,128)S(1)} %bitcast.10), kind=kLoop, calls=%fused_computation | loop fusion | flops 65536 | bytes 532480 | tf_op jit(solution)/shard_map/mul | solution.py:518

commit v6 on v5

--- a/solution.py
+++ b/solution.py
@@ -76,16 +76,19 @@
     signal(barrier, (gx, gy, 1 - gz))
     for step in (1, -1, 2, -2):
         signal(barrier, ring(step))
-    for _, solver in axes[0]["solvers"]:
-        pl.when(gx != solver)(functools.partial(signal, barrier, axes[0]["device"](solver)))
 
     @pl.when(axes[0]["solves"])
     def _():
-        @pl.loop(0, N)
-        def _(i):
-            pl.when(i != gx)(lambda: signal(barrier, axes[0]["device"](i)))
-
-    expected = 5 + jnp.where(axes[0]["solves"], N - 1 + 2 * SOLVERS - 1, 2 * SOLVERS)
+        @pl.loop(1, N)
+        def _(step):
+            signal(barrier, axes[0]["device"](lax.rem(gx + step, N)))
+
+    @pl.when(jnp.logical_not(axes[0]["solves"]))
+    def _():
+        for _, solver in axes[0]["solvers"]:
+            signal(barrier, axes[0]["device"](solver))
+
+    expected = 5 + jnp.where(axes[0]["solves"], N - 1, 2 * SOLVERS)
 
     def tell(r):
         signal(far_sem.at[r], ring(2 << r))
@@ -342,7 +345,6 @@
     z_copy[0].start()
     pl.when(gy < N - 1)(y_up.start)
     pl.when(gy > 0)(y_down.start)
-    to_solvers(0, coef_send, coef_recv, 0)
     tell(0)
 
     weights(0, along, cfl_x)
@@ -375,6 +377,8 @@
             edge_coef[0] = west
         if y == N - 1:
             edge_coef[1] = east
+
+    to_solvers(0, coef_send, coef_recv, 0)
 
     factor(1, across, cfl_y)
     weights(1, across, cfl_y)

time: 39.9 us -> 39.3 us (0.985)
  the two profiles are of different devices: /device:TPU:1 before, /device:TPU:32 now
where the time goes in v6:
time: 39.3 us; the launch traced here: 39.2 us
  Pallas kernels  37.8 us (96%)
  other arithmetic  0.72 us (2%)
  between operations  0.64 us (2%)
    pallas_call x1, Pallas kernels, body(): pl.pallas_call(kernel, out_shape=[jax.ShapeDtypeStruct(block, F32)] * 2 +...  37.8 us

profile of v6, /device:TPU:32, one launch (start us, length us, event | category | flops | bytes accessed | tf_op | source)
XLA Modules:
  0.0 39.2 jit_solution(3561146744325829365)
XLA Ops:
  0.6 37.8 %shard_map.95 = (f32[256,128]{1,0:T(8,128)S(1)}, f32[256,128]{1,0:T(8,128)S(1)}, f32[16,128]{1,0:T(8,128)S(1)}) custom-call(f32[256,128]{1,0:T(8,128)} %bitcast.12, f32[256,128]{1,0:T(8,128)} %bitcast.13, f32[256,128]{1,0:T(8,128)} %bitcast.14, f32[256,128]{1,0:T(8,128)} %bitcast.15, f32[256,128]{1,0:T(8,128)} %bitcast.16, f32[256,128]{1,0:T(8,128)} %bitcast.17, ...), custom_call_target="tpu_custom_call" | custom-call | tf_op jit(solution)/shard_map/pallas_call | solution.py:494
  38.5 0.7 %broadcast_multiply_fusion = (f32[16,16,128]{2,1,0:T(8,128)}, f32[16,16,128]{2,1,0:T(8,128)}) fusion(f32[16,16,128]{2,1,0:T(8,128)S(1)} %bitcast.11, f32[16,128]{1,0:T(8,128)S(1)} %get-tuple-element.6, f32[16,16,128]{2,1,0:T(8,128)S(1)} %bitcast.10), kind=kLoop, calls=%fused_computation | loop fusion | flops 65536 | bytes 532480 | tf_op jit(solution)/shard_map/mul | solution.py:522

commit v7 on v6

--- a/solution.py
+++ b/solution.py
@@ -32,9 +32,10 @@
     half_x, chip_x = lax.div(gx, N // 2), lax.rem(lax.div(gx, 2), 4)
     odd = lax.rem(gy + core, 2)
 
-    def solver_x(other_half, step):
-        chip = lax.rem(chip_x + step, 4)
-        return chip, N // 2 * lax.rem(half_x + other_half, 2) + 2 * chip
+    def solver_x(other_half, step, other_core):
+        c = lax.rem(core + other_core, 2)
+        j = N // 2 * lax.rem(half_x + other_half, 2) + 2 * lax.rem(chip_x + step, 4) + c
+        return lax.rem(j, 4), j
 
     def solver_y(step):
         j = lax.rem(gy + step - odd + N, N)
@@ -42,12 +43,12 @@
 
     axes = (
         dict(
-            me=gx, tile=chip_x, solves=core == 0, device=lambda i: (i, gy, gz),
-            solvers=[solver_x(*step) for step in ((1, 2), (1, 1), (1, 3), (0, 2), (1, 0), (0, 1), (0, 3), (0, 0))],
-            served=[
-                N // 2 * half_x + 2 * lax.rem(chip_x + step, 4) + c
-                for step, c in ((2, 1), (2, 0), (1, 1), (3, 1), (1, 0), (3, 0), (0, 1))
+            me=gx, tile=lax.rem(gx, 4), solves=gx >= 0, device=lambda i: (i, gy, gz),
+            solvers=[
+                solver_x(*step, c)
+                for step in ((1, 2), (1, 1), (1, 3), (0, 2), (1, 0), (0, 1), (0, 3), (0, 0)) for c in (1, 0)
             ],
+            served=[4 * lax.div(gx, 4) + lax.rem(gx + step, 4) for step in (2, 3, 1)],
         ),
         dict(
             me=gy, tile=lax.rem(lax.div(gy, 2), 4), solves=odd == 0, device=lambda i: (gx, i, gz),
@@ -77,18 +78,11 @@
     for step in (1, -1, 2, -2):
         signal(barrier, ring(step))
 
-    @pl.when(axes[0]["solves"])
-    def _():
-        @pl.loop(1, N)
-        def _(step):
-            signal(barrier, axes[0]["device"](lax.rem(gx + step, N)))
-
-    @pl.when(jnp.logical_not(axes[0]["solves"]))
-    def _():
-        for _, solver in axes[0]["solvers"]:
-            signal(barrier, axes[0]["device"](solver))
-
-    expected = 5 + jnp.where(axes[0]["solves"], N - 1, 2 * SOLVERS)
+    @pl.loop(1, N)
+    def _(step):
+        signal(barrier, axes[0]["device"](lax.rem(gx + step, N)))
+
+    expected = 5 + N - 1
 
     def tell(r):
         signal(far_sem.at[r], ring(2 << r))
@@ -199,7 +193,8 @@
         pltpu.make_async_copy(ref.at[pl.ds(0, count)], ref.at[pl.ds(0, count)], sem).wait()
 
     def sent_to_solvers(d, send, kind):
-        wait_slots(send.at[d], SOLVERS, net_sem.at[d, kind, 0])
+        for _ in range(len(axes[d]["solvers"]) // SOLVERS - 1):
+            wait_slots(send.at[d], SOLVERS, net_sem.at[d, kind, 0])
         pl.when(axes[d]["solves"])(
             lambda: wait_slots(send.at[d], SOLVERS - 1, net_sem.at[d, kind, 0])
         )

time: 39.3 us -> 39.3 us (level)
  the two profiles are of different devices: /device:TPU:32 before, /device:TPU:24 now
where the time goes in v7:
time: 39.3 us; the launch traced here: 38.6 us
  Pallas kernels  37.3 us (95%)
  other arithmetic  0.72 us (2%)
  between operations  0.64 us (2%)
    pallas_call x1, Pallas kernels, body(): pl.pallas_call(kernel, out_shape=[jax.ShapeDtypeStruct(block, F32)] * 2 +...  37.3 us

profile of v7, /device:TPU:24, one launch (start us, length us, event | category | flops | bytes accessed | tf_op | source)
XLA Modules:
  0.0 38.6 jit_solution(7362640459652516516)
XLA Ops:
  0.6 37.3 %shard_map.95 = (f32[256,128]{1,0:T(8,128)S(1)}, f32[256,128]{1,0:T(8,128)S(1)}, f32[16,128]{1,0:T(8,128)S(1)}) custom-call(f32[256,128]{1,0:T(8,128)} %bitcast.12, f32[256,128]{1,0:T(8,128)} %bitcast.13, f32[256,128]{1,0:T(8,128)} %bitcast.14, f32[256,128]{1,0:T(8,128)} %bitcast.15, f32[256,128]{1,0:T(8,128)} %bitcast.16, f32[256,128]{1,0:T(8,128)} %bitcast.17, ...), custom_call_target="tpu_custom_call" | custom-call | tf_op jit(solution)/shard_map/pallas_call | solution.py:489
  37.9 0.7 %broadcast_multiply_fusion = (f32[16,16,128]{2,1,0:T(8,128)}, f32[16,16,128]{2,1,0:T(8,128)}) fusion(f32[16,16,128]{2,1,0:T(8,128)S(1)} %bitcast.11, f32[16,128]{1,0:T(8,128)S(1)} %get-tuple-element.6, f32[16,16,128]{2,1,0:T(8,128)S(1)} %bitcast.10), kind=kLoop, calls=%fused_computation | loop fusion | flops 65536 | bytes 532480 | tf_op jit(solution)/shard_map/mul | solution.py:517
